TPU v7x, 256 devices: a whole 4x4x8 slice. The times are simulated.
256 devices in a mesh: row: 4 (over z_hi), col: 8 (over y, z_lo), depth: 8 (over x, core).
Axes of the slice: x: 4, y: 4, z: 8 (z_hi: 4, z_lo: 2; z = z_hi * 2 + z_lo), core: 2. Of those that a mesh axis runs over, the one named last changes fastest.
Arguments:
- tokens: bfloat16 [4096, 6144], P(('depth', 'col'), 'row'), may hold values from -20 to 20
- projection_weight: bfloat16 [6144, 24576], P('row', 'col'), may hold values from -0.078125 to 0.078125
- projection_bias: bfloat16 [24576], P('col'), may hold values from -3 to 3
- layer_norm_gain: bfloat16 [6144], P('row'), may hold values from 0.5 to 1.5
- layer_norm_shift: bfloat16 [6144], P('row'), may hold values from -2 to 2
- adapter_down_weight: float32 [32, 6144], P(None, ('row', 'depth')), may hold values from -0.078125 to 0.078125
- adapter_up_weight: float32 [32, 24576], P(None, ('col', 'depth')), may hold values from -0.3 to 0.3
- down_first_moment: float32 [32, 6144], P(None, ('row', 'depth')), may hold values from -300 to 300
- down_second_moment: float32 [32, 6144], P(None, ('row', 'depth')), may hold values from 100 to 10000
- up_first_moment: float32 [32, 24576], P(None, ('col', 'depth')), may hold values from -60 to 60
- up_second_moment: float32 [32, 24576], P(None, ('col', 'depth')), may hold values from 10 to 1000
- cotangent: bfloat16 [4096, 24576], P(('depth', 'row'), 'col'), may hold values from -6 to 6
Outputs:
- hidden: bfloat16 [4096, 24576], P(('depth', 'row'), 'col')
- input_grad: bfloat16 [4096, 6144], P(('depth', 'col'), 'row')
- fresh_down_weight: float32 [32, 6144], P(None, ('row', 'depth'))
- fresh_down_first_moment: float32 [32, 6144], P(None, ('row', 'depth'))
- fresh_down_second_moment: float32 [32, 6144], P(None, ('row', 'depth'))
- fresh_up_weight: float32 [32, 24576], P(None, ('col', 'depth'))
- fresh_up_first_moment: float32 [32, 24576], P(None, ('col', 'depth'))
- fresh_up_second_moment: float32 [32, 24576], P(None, ('col', 'depth'))
All inputs are finite; a program needn't handle non-finite values.
Results may differ from a plain program's by a relative error of at most 0.002.
The roundings to bfloat16 on the way count: a program that leaves them out, or rounds other values in their place, can miss the bound.
Values may be sent and summed in bfloat16 or wider, within the bound.
A program may use at most 128 MiB of HBM per device.

v0:
```python
import jax
import jax.numpy as jnp
from jax import lax
from jax.sharding import PartitionSpec as P

adapter_scale = 0.5
norm_epsilon = 1e-05
beta_first = 0.9
beta_second = 0.999
adam_step = 10
learn_rate = 0.01
decay_rate = 0.1
adam_epsilon = 1e-08


def gelu_slope(values):
    inner = 0.7978845608 * (values + 0.044715 * values * values * values)
    tangent = jnp.tanh(inner)
    return 0.5 * (1.0 + tangent) + 0.5 * values * (1.0 - tangent * tangent) * 0.7978845608 * (
        1.0 + 3.0 * 0.044715 * values * values
    )


def decoupled_adam_update(weights_now, moment, square, gradient):
    new_moment = beta_first * moment + (1.0 - beta_first) * gradient
    new_square = beta_second * square + (1.0 - beta_second) * gradient * gradient
    update = (
        new_moment
        / (1.0 - beta_first**adam_step)
        / (jnp.sqrt(new_square / (1.0 - beta_second**adam_step)) + adam_epsilon)
    )
    return (weights_now - learn_rate * (update + decay_rate * weights_now), new_moment, new_square)


def shards(
    tokens,
    projection_weight,
    projection_bias,
    layer_norm_gain,
    layer_norm_shift,
    adapter_down_weight,
    adapter_up_weight,
    down_first_moment,
    down_second_moment,
    up_first_moment,
    up_second_moment,
    cotangent,
):
    highest_precision = lax.Precision.HIGHEST
    feature_count = tokens.shape[1] * lax.axis_size("row")
    values = tokens.astype(jnp.float32)
    local_stats = (jnp.sum(values, axis=1), jnp.sum(values * values, axis=1))
    value_total, square_total = lax.psum((local_stats[0], local_stats[1]), "row")
    mean_value = (value_total / feature_count)[:, None]
    inv_std = lax.rsqrt(
        square_total[:, None] / feature_count - mean_value * mean_value + norm_epsilon
    )
    centred = (values - mean_value) * inv_std
    normalized_input = (centred * layer_norm_gain + layer_norm_shift).astype(jnp.bfloat16)
    slice_normed = lax.all_gather(normalized_input, "col", axis=0, tiled=True)
    down_weight_block, up_weight_block = (
        lax.all_gather(adapter_down_weight, "depth", axis=1, tiled=True),
        lax.all_gather(adapter_up_weight, "depth", axis=1, tiled=True),
    )
    down_partial = down_weight_block.astype(jnp.bfloat16)
    up_partial = up_weight_block.astype(jnp.bfloat16)
    adapter_output = lax.dot_general(
        slice_normed, down_partial, (((1,), (1,)), ((), ())), preferred_element_type=jnp.float32
    )
    main_part = jnp.dot(
        slice_normed, projection_weight, preferred_element_type=jnp.float32
    ) + adapter_scale * jnp.dot(adapter_output, up_weight_block, precision=highest_precision)
    pre_sum, rank_projection = (
        lax.psum_scatter(main_part, "row", scatter_dimension=0, tiled=True),
        lax.psum_scatter(adapter_output, "row", scatter_dimension=0, tiled=True),
    )
    preactivation_value = pre_sum + projection_bias
    activation_slopes = (cotangent.astype(jnp.float32) * gelu_slope(preactivation_value)).astype(
        jnp.bfloat16
    )
    slice_slopes = lax.all_gather(activation_slopes, "row", axis=0, tiled=True)
    hidden = jax.nn.gelu(preactivation_value, approximate=True).astype(jnp.bfloat16)
    adapter_backward = lax.dot_general(
        slice_slopes, up_partial, (((1,), (1,)), ((), ())), preferred_element_type=jnp.float32
    )
    back_part = lax.dot_general(
        slice_slopes,
        projection_weight,
        (((1,), (1,)), ((), ())),
        preferred_element_type=jnp.float32,
    ) + adapter_scale * jnp.dot(adapter_backward, down_weight_block, precision=highest_precision)
    normalized_gradient = lax.psum_scatter(back_part, "col", scatter_dimension=0, tiled=True)
    scaled = normalized_gradient * layer_norm_gain
    scaled_total, product_total = lax.psum(
        (jnp.sum(scaled, axis=1), jnp.sum(scaled * centred, axis=1)), "row"
    )
    input_grad = (
        inv_std
        * (
            scaled
            - (scaled_total / feature_count)[:, None]
            - centred * (product_total / feature_count)[:, None]
        )
    ).astype(jnp.bfloat16)
    up_contribution = adapter_scale * jnp.dot(
        rank_projection.T, activation_slopes.astype(jnp.float32), precision=highest_precision
    )
    down_contribution = adapter_scale * jnp.dot(
        adapter_backward.T, slice_normed.astype(jnp.float32), precision=highest_precision
    )
    up_depth, down_depth = (
        lax.psum_scatter(up_contribution, "depth", scatter_dimension=1, tiled=True),
        lax.psum_scatter(down_contribution, "depth", scatter_dimension=1, tiled=True),
    )
    up_gradient = lax.psum(up_depth, "row")
    down_gradient = lax.psum(down_depth, "col")
    fresh_down_weight, fresh_down_first_moment, fresh_down_second_moment = decoupled_adam_update(
        adapter_down_weight, down_first_moment, down_second_moment, down_gradient
    )
    fresh_up_weight, fresh_up_first_moment, fresh_up_second_moment = decoupled_adam_update(
        adapter_up_weight, up_first_moment, up_second_moment, up_gradient
    )
    return (
        hidden,
        input_grad,
        fresh_down_weight,
        fresh_down_first_moment,
        fresh_down_second_moment,
        fresh_up_weight,
        fresh_up_first_moment,
        fresh_up_second_moment,
    )


def solution(mesh):
    placed = (
        P(("depth", "col"), "row"),
        P("row", "col"),
        P("col"),
        P("row"),
        P("row"),
        P(None, ("row", "depth")),
        P(None, ("col", "depth")),
        P(None, ("row", "depth")),
        P(None, ("row", "depth")),
        P(None, ("col", "depth")),
        P(None, ("col", "depth")),
        P(("depth", "row"), "col"),
    )
    return jax.shard_map(
        shards,
        mesh=mesh,
        in_specs=placed,
        out_specs=(
            P(("depth", "row"), "col"),
            P(("depth", "col"), "row"),
            P(None, ("row", "depth")),
            P(None, ("row", "depth")),
            P(None, ("row", "depth")),
            P(None, ("col", "depth")),
            P(None, ("col", "depth")),
            P(None, ("col", "depth")),
        ),
        check_vma=False,
    )
```

profile of v0, /device:TPU:8, one launch (start us, length us, event | category | flops | bytes accessed | tf_op | source)
XLA Modules:
  0.0 479.9 jit_solution(1620494768978060856)
XLA Ops:
  9.7 14.9 %all-reduce.1 = (f32[64]{0:T(128)S(1)}, f32[64]{0:T(128)S(1)}) all-reduce(f32[64]{0:T(128)S(1)} %get-tuple-element.11, f32[64]{0:T(128)S(1)} %get-tuple-element.10), channel_id=1, replica_groups=mesh['row'=4,'col'=8,'depth'=8] {'row'}, use_global_device_ids=true, to_apply=%region_3.0 | all-reduce | flops 128 | bytes 1024 | tf_op jit(solution)/shard_map/psum | solution.py:53
  24.6 1.8 fusion.21
  26.4 13.4 %all-gather = f32[8,192,32]{1,2,0:T(8,128)S(1)} all-gather(f32[1,192,32]{1,2,0:T(8,128)} %bitcast.22), channel_id=1, replica_groups=mesh['row'=4,'col'=8,'depth'=8] {'depth'}, dimensions={0}, use_global_device_ids=true | all-gather | bytes 221184 | tf_op jit(solution)/shard_map/all_gather | solution.py:62
  40.1 13.0 %all_gather.14 = f32[32,3072]{1,0:T(8,128)S(1)} all-gather(f32[32,384]{1,0:T(8,128)S(1)} %copy-done.6), channel_id=1, replica_groups=mesh['row'=4,'col'=8,'depth'=8] {'depth'}, dimensions={1}, use_global_device_ids=true | all-gather | bytes 442368 | tf_op jit(solution)/shard_map/all_gather | solution.py:63
  53.1 15.8 %all-gather.4.cloned.1.call-done = bf16[512,1536]{1,0:T(8,128)(2,1)} async-done(((bf16[64,1536]{1,0:T(8,128)(2,1)}), bf16[512,1536]{1,0:T(8,128)(2,1)}) %all-gather.4.cloned.1.call-update) | async-done | bytes 1572880 | tf_op jit(solution)/shard_map/all_gather | solution.py:60
  68.9 2.1 fusion.29
  71.0 7.6 %fusion.35 = f32[512,3072]{1,0:T(8,128)S(1)} fusion(bf16[512,1536]{1,0:T(8,128)(2,1)S(1)} %copy-done.2, bf16[1536,3072]{1,0:T(8,128)(2,1)} %param.13), kind=kOutput, calls=%fused_computation.54 | convolution fusion | flops 4831838208 | bytes 17301504 | tf_op jit(solution)/shard_map/dot_general | solution.py:70
  78.6 7.2 %multiply_add_fusion = f32[512,3072]{1,0:T(8,128)} fusion(f32[512,3072]{1,0:T(8,128)S(1)} %fusion.35, f32[512,32]{0,1:T(8,128)S(1)} %fusion.29, f32[32,3072]{1,0:T(8,128)S(1)} %all_gather.14), kind=kOutput, calls=%fused_computation | convolution fusion | flops 607125504 | bytes 13041664 | tf_op jit(solution)/shard_map/dot_general | solution.py:72
  86.5 118.7 %reduce-scatter.8.cloned.1.call-done = f32[128,3072]{1,0:T(8,128)} async-done(((f32[512,3072]{1,0:T(8,128)}), f32[128,3072]{1,0:T(8,128)}) %reduce-scatter.8.cloned.1.call-update) | async-done | bytes 1572880 | tf_op jit(solution)/shard_map/reduce_scatter | solution.py:74
  205.2 4.1 fusion.15
  210.0 61.1 %all-gather.6.cloned.1.call-done = bf16[512,3072]{1,0:T(8,128)(2,1)} async-done(((bf16[128,3072]{1,0:T(8,128)(2,1)}), bf16[512,3072]{1,0:T(8,128)(2,1)}) %all-gather.6.cloned.1.call-update) | async-done | bytes 3145744 | tf_op jit(solution)/shard_map/all_gather | solution.py:81
  271.1 2.9 fusion.27
  274.0 3.1 convolution_multiply_fusion.2
  277.1 2.1 copy.22
  279.5 7.7 %fusion.36 = f32[512,1536]{1,0:T(8,128)S(1)} fusion(bf16[512,3072]{1,0:T(8,128)(2,1)S(1)} %copy-done, bf16[1536,3072]{1,0:T(8,128)(2,1)} %param.13), kind=kOutput, calls=%fused_computation.55 | convolution fusion | flops 4831838208 | bytes 15728640 | tf_op jit(solution)/shard_map/dot_general | solution.py:86
  287.1 4.5 fusion
  291.8 11.2 %reduce-scatter.12.cloned.1.call-done = f32[128,32]{0,1:T(8,128)} async-done(((f32[512,32]{0,1:T(8,128)}), f32[128,32]{0,1:T(8,128)}) %reduce-scatter.12.cloned.1.call-update) | async-done | bytes 16400 | tf_op jit(solution)/shard_map/reduce_scatter | solution.py:75
  303.0 1.9 convolution_multiply_fusion
  304.9 32.5 %reduce-scatter.16.cloned.1.call-done = f32[192,32]{1,0:T(8,128)} async-done(((f32[1536,32]{1,0:T(8,128)}), f32[192,32]{1,0:T(8,128)}) %reduce-scatter.16.cloned.1.call-update) | async-done | bytes 24592
  338.3 33.6 %psum.46 = f32[32,192]{1,0:T(8,128)S(1)} all-reduce(f32[32,192]{1,0:T(8,128)S(1)} %copy.23), channel_id=1, replica_groups=mesh['row'=4,'col'=8,'depth'=8] {'col'}, use_global_device_ids=true, to_apply=%region_11.0 | all-reduce | flops 6144 | bytes 49152 | tf_op jit(solution)/shard_map/psum | solution.py:116
  372.6 39.7 %reduce-scatter.10.cloned.1.call-done = f32[64,1536]{1,0:T(8,128)} async-done(((f32[512,1536]{1,0:T(8,128)}), f32[64,1536]{1,0:T(8,128)}) %reduce-scatter.10.cloned.1.call-update) | async-done | bytes 393232 | tf_op jit(solution)/shard_map/reduce_scatter | solution.py:92
  413.6 35.3 %reduce-scatter.14.cloned.1.call-done = f32[32,384]{1,0:T(8,128)} async-done(((f32[32,3072]{1,0:T(8,128)}), f32[32,384]{1,0:T(8,128)}) %reduce-scatter.14.cloned.1.call-update) | async-done | bytes 49168 | tf_op jit(solution)/shard_map/reduce_scatter | solution.py:112
  449.0 21.5 %all-reduce = (f32[64]{0:T(128)S(1)}, f32[64]{0:T(128)S(1)}, f32[32,384]{1,0:T(8,128)S(1)}) all-reduce(f32[64]{0:T(128)S(1)} %get-tuple-element.9, f32[64]{0:T(128)S(1)} %get-tuple-element.8, f32[32,384]{1,0:T(8,128)} %reduce-scatter.14.cloned.1.call-done), channel_id=1, replica_groups=mesh['row'=4,'col'=8,'depth'=8] {'row'}, use_global_device_ids=true, to_apply=%region_9.0 | all-reduce | flops 12416 | bytes 99328 | tf_op jit(solution)/shard_map/psum | solution.py:94
  471.2 1.9 fusion.25
  (52 shorter events, 8.1 us)
Async XLA Ops:
  7.2 32.9 %copy-start.6 = (f32[32,384]{1,0:T(8,128)S(1)}, f32[32,384]{1,0:T(8,128)}, u32[]{:S(2)}) copy-start(f32[32,384]{1,0:T(8,128)} %param.18) | copy-start | bytes 147460
  7.2 61.7 %all-gather.4.cloned.1.call-start = ((), (), s32[]{:S(2)}) async-start(), calls=%async_computation.5 | async-start | bytes 1769472 | tf_op jit(solution)/shard_map/all_gather | solution.py:60
  26.4 178.8 %reduce-scatter.8.cloned.1.call-start = ((), (), s32[]{:S(2)}) async-start(), calls=%async_computation.6 | async-start | bytes 7864320 | tf_op jit(solution)/shard_map/reduce_scatter | solution.py:74
  68.9 2.1 copy-start.2
  70.9 7.6 %copy-start.5 = (f32[512,32]{0,1:T(8,128)}, f32[512,32]{0,1:T(8,128)S(1)}, u32[]{:S(2)}) copy-start(f32[512,32]{0,1:T(8,128)S(1)} %fusion.29) | copy-start | bytes 196612
  85.8 0.7 copy-start.12
  85.8 119.4 %copy-start.4 = (bf16[128,3072]{1,0:T(8,128)(2,1)S(1)}, bf16[128,3072]{1,0:T(8,128)(2,1)}, u32[]{:S(2)}) copy-start(bf16[128,3072]{1,0:T(8,128)(2,1)} %param.23) | copy-start | bytes 2359300
  85.8 185.3 %all-gather.6.cloned.1.call-start = ((), (), s32[]{:S(2)}) async-start(), calls=%async_computation.7 | async-start | bytes 3932160 | tf_op jit(solution)/shard_map/all_gather | solution.py:81
  209.3 93.6 %reduce-scatter.12.cloned.1.call-start = ((), (), s32[]{:S(2)}) async-start(), calls=%async_computation.9 | async-start | bytes 81920 | tf_op jit(solution)/shard_map/reduce_scatter | solution.py:75
  209.9 127.4 %reduce-scatter.16.cloned.1.call-start = ((), (), s32[]{:S(2)}) async-start(), calls=%async_computation.11 | async-start | bytes 884736
  274.0 5.5 %copy-start = (bf16[512,3072]{1,0:T(8,128)(2,1)S(1)}, bf16[512,3072]{1,0:T(8,128)(2,1)}, u32[]{:S(2)}) copy-start(bf16[512,3072]{1,0:T(8,128)(2,1)} %all-gather.6.cloned.1.call-done) | copy-start | bytes 9437188
  279.2 133.1 %reduce-scatter.10.cloned.1.call-start = ((), (), s32[]{:S(2)}) async-start(), calls=%async_computation.8 | async-start | bytes 3538944 | tf_op jit(solution)/shard_map/reduce_scatter | solution.py:92
  291.6 11.4 %copy-start.1 = (bf16[128,3072]{1,0:T(8,128)(2,1)S(1)}, bf16[128,3072]{1,0:T(8,128)(2,1)}, u32[]{:S(2)}) copy-start(bf16[128,3072]{1,0:T(8,128)(2,1)} %get-tuple-element.23) | copy-start | bytes 2359300
  291.6 80.3 %copy-start.7 = (f32[32,192]{1,0:T(8,128)S(1)}, f32[32,192]{1,0:T(8,128)}, u32[]{:S(2)}) copy-start(f32[32,192]{1,0:T(8,128)} %param.17) | copy-start | bytes 73732
  291.7 80.3 %copy-start.10 = (f32[32,192]{1,0:T(8,128)S(1)}, f32[32,192]{1,0:T(8,128)}, u32[]{:S(2)}) copy-start(f32[32,192]{1,0:T(8,128)} %param.19) | copy-start | bytes 73732
  291.7 80.3 %copy-start.11 = (f32[32,192]{1,0:T(8,128)S(1)}, f32[32,192]{1,0:T(8,128)}, u32[]{:S(2)}) copy-start(f32[32,192]{1,0:T(8,128)} %param.20) | copy-start | bytes 73732
  291.7 120.7 %copy-start.3 = (bf16[64,1536]{1,0:T(8,128)(2,1)S(1)}, bf16[64,1536]{1,0:T(8,128)(2,1)}, u32[]{:S(2)}) copy-start(bf16[64,1536]{1,0:T(8,128)(2,1)} %param.12) | copy-start | bytes 589828
  291.7 178.8 %copy-start.8 = (f32[32,384]{1,0:T(8,128)S(1)}, f32[32,384]{1,0:T(8,128)}, u32[]{:S(2)}) copy-start(f32[32,384]{1,0:T(8,128)} %param.21) | copy-start | bytes 147460
  291.7 178.8 %copy-start.9 = (f32[32,384]{1,0:T(8,128)S(1)}, f32[32,384]{1,0:T(8,128)}, u32[]{:S(2)}) copy-start(f32[32,384]{1,0:T(8,128)} %param.22) | copy-start | bytes 147460
  291.7 157.2 %reduce-scatter.14.cloned.1.call-start = ((), (), s32[]{:S(2)}) async-start(), calls=%async_computation.10 | async-start | bytes 442368 | tf_op jit(solution)/shard_map/reduce_scatter | solution.py:112
Sparse Core Ops, SparseCore 0:
  26.5 42.3 all-gather.3
  85.9 119.2 reduce-scatter.7
  209.5 61.5 all-gather.5
  273.4 29.5 reduce-scatter.11
  305.5 31.7 reduce-scatter.15
  339.8 72.5 reduce-scatter.9
  414.9 34.0 reduce-scatter.13
where the time goes:
time: 480 us
  waiting for transfers between devices  315 us (66%)
  blocking collectives  96.4 us (20%)
  matrix products  36.9 us (8%)
  between operations  14.3 us (3%)
  other arithmetic  12.8 us (3%)
    reduce_scatter x1, waiting for transfers between devices, shards(): lax.psum_scatter(main_part, 'row', scatter_dimension=0, tiled=True)  119 us
    all_gather x1, waiting for transfers between devices, shards(): slice_slopes = lax.all_gather(activation_slopes, 'row', axis=0, tiled=True)  61.1 us
    reduce_scatter x1, waiting for transfers between devices, shards(): lax.psum_scatter(back_part, 'col', scatter_dimension=0, tiled=True)  39.7 us
    reduce_scatter x1, waiting for transfers between devices, shards(): lax.psum_scatter(up_contribution, 'depth', scatter_dimension=1, tiled=True)  35.3 us
    psum x1, blocking collectives, shards(): down_gradient = lax.psum(down_depth, 'col')  33.6 us
    unnamed x8, waiting for transfers between devices  33.1 us
    psum x1, blocking collectives, shards(): lax.psum((jnp.sum(scaled, axis=1), jnp.sum(scaled * centred, axis=1)), 'r...  21.5 us
    all_gather x1, waiting for transfers between devices, shards(): slice_normed = lax.all_gather(normalized_input, 'col', axis=0, tiled=True)  15.8 us
  transfers between devices with their start and end apart: 7, of which 7 were waited for; matrix products, arithmetic and copies ran while one was open for 5% of the time, Pallas kernels for 0%

commit v1 on v0

v1 whole, which is shorter than its diff:
```python
import functools
import jax
import jax.numpy as jnp
from jax import lax
from jax.experimental import pallas as pl
from jax.experimental.pallas import tpu as pltpu
from jax.sharding import PartitionSpec as P

adapter_scale = 0.5
norm_epsilon = 1e-05
beta_first = 0.9
beta_second = 0.999
adam_step = 10
learn_rate = 0.01
decay_rate = 0.1
adam_epsilon = 1e-08

f32 = jnp.float32
bf16 = jnp.bfloat16
MESH = pl.DeviceIdType.MESH
NT = (((1,), (1,)), ((), ()))

ROWS, COLS, DEPTH = 4, 8, 8
YS = COLS // 2
CHUNKS = 4
OWN = 64
STEP = OWN // CHUNKS
TOK = STEP * COLS
FEAT, HID, RANK = 1536, 3072, 32
UPB, DNB = HID // DEPTH, FEAT // DEPTH
RING = 2 * STEP
CODE_SPAN = 120.0
LN2 = 0.6931471805599453
TILE = 512


def gelu_both(v):
    inner = 0.7978845608 * (v + 0.044715 * v * v * v)
    tangent = jnp.tanh(inner)
    value = 0.5 * v * (1.0 + tangent)
    slope = 0.5 * (1.0 + tangent) + 0.5 * v * (1.0 - tangent * tangent) * 0.7978845608 * (
        1.0 + 3.0 * 0.044715 * v * v
    )
    return value, slope


def adam(weight, moment, square, gradient):
    new_moment = beta_first * moment + (1.0 - beta_first) * gradient
    new_square = beta_second * square + (1.0 - beta_second) * gradient * gradient
    update = (
        new_moment
        / (1.0 - beta_first**adam_step)
        / (jnp.sqrt(new_square / (1.0 - beta_second**adam_step)) + adam_epsilon)
    )
    return weight - learn_rate * (update + decay_rate * weight), new_moment, new_square


def encode(load, store, rows, width):
    top = jnp.zeros((rows, 1), f32)
    for t in range(0, width, TILE):
        top = jnp.maximum(top, jnp.max(jnp.abs(load(t)), axis=1, keepdims=True))
    top = (jnp.maximum(top, 1e-30) * 1.01).astype(bf16)
    factor = CODE_SPAN / top.astype(f32)
    for t in range(0, width, TILE):
        store(t, TILE, jnp.exp2(load(t) * factor).astype(bf16))
    store(width, 128, jnp.broadcast_to(top, (rows, 128)))


def decoder(load, width):
    scale = load(width, 128)[:, 0:1].astype(f32) * (1.0 / (CODE_SPAN * LN2))
    return lambda t: jnp.log(load(t, TILE).astype(f32)) * scale


def kernel(
    tok,
    w_hbm,
    bias,
    gain,
    shift,
    down_w,
    up_w,
    down_m,
    down_s,
    up_m,
    up_s,
    cot_hbm,
    hidden,
    input_grad,
    new_down_w,
    new_down_m,
    new_down_s,
    new_up_w,
    new_up_m,
    new_up_s,
    w,
    cot,
    local_sem,
    stat_s,
    stat_r,
    cen,
    istd,
    nrm,
    upg,
    dng,
    d_low,
    d_prod,
    u_low,
    u_prod,
    part,
    low,
    rs_s,
    rs_r,
    slg,
    back,
    cs_s,
    cs_r,
    lo_s,
    lo_r,
    ng,
    gst_s,
    gst_r,
    up_acc,
    dn_acc,
    ugs,
    ugr,
    dgs,
    dgr,
    upx,
    dnx,
    stat_sem,
    nlo_sem,
    nown_sem,
    nfwd_sem,
    upg_sem,
    dng_sem,
    rs_sem,
    ag_sem,
    cs_sem,
    lo_sem,
    gst_sem,
    ug_sem,
    dg_sem,
    ux_sem,
    dx_sem,
):
    r = lax.axis_index("row")
    c = lax.axis_index("col")
    d = lax.axis_index("depth")
    y, lo = c // 2, c % 2
    right, left, opp = (r + 1) % ROWS, (r + 3) % ROWS, (r + 2) % ROWS
    pc = y * 2 + (1 - lo)

    def remote(src, dst, sems, index, device):
        return pltpu.make_async_remote_copy(
            src_ref=src,
            dst_ref=dst,
            send_sem=sems.at[(0,) + index],
            recv_sem=sems.at[(1,) + index],
            device_id=device,
            device_id_type=MESH,
        )

    w_copy = pltpu.make_async_copy(w_hbm, w, local_sem.at[0])
    cot_copy = pltpu.make_async_copy(cot_hbm, cot, local_sem.at[1])
    w_copy.start()
    cot_copy.start()

    barrier = pltpu.get_barrier_semaphore()
    for j in range(1, ROWS):
        pl.semaphore_signal(barrier, inc=1, device_id={"row": (r + j) % ROWS}, device_id_type=MESH)
    for j in range(1, COLS):
        pl.semaphore_signal(barrier, inc=1, device_id={"col": (c + j) % COLS}, device_id_type=MESH)
    for j in range(1, DEPTH):
        pl.semaphore_signal(
            barrier, inc=1, device_id={"depth": (d + j) % DEPTH}, device_id_type=MESH
        )

    x = tok[...].astype(f32)
    lane = lax.broadcasted_iota(jnp.int32, (OWN, 128), 1)
    s1 = jnp.sum(x, axis=1, keepdims=True)
    s2 = jnp.sum(x * x, axis=1, keepdims=True)
    stat_s[...] = jnp.where(lane == 0, s1, jnp.where(lane == 1, s2, 0.0))
    upg[d] = up_w[...]
    dng[d] = down_w[...]
    pl.semaphore_wait(barrier, ROWS + COLS + DEPTH - 3)

    def stat_copy(j):
        return remote(stat_s, stat_r.at[j - 1], stat_sem, (j,), {"row": (r + j) % ROWS})

    def upg_copy(j, owner):
        return remote(upg.at[owner], upg.at[owner], upg_sem, (j,), {"depth": (d + j) % DEPTH})

    def dng_copy(j, owner):
        return remote(dng.at[owner], dng.at[owner], dng_sem, (j,), {"depth": (d + j) % DEPTH})

    for j in range(1, ROWS):
        stat_copy(j).start()
    for j in range(1, DEPTH):
        dng_copy(j, d).start()
        upg_copy(j, d).start()
    for j in range(1, ROWS):
        stat_copy(j).wait_recv()
    total = stat_s[...] + stat_r[0] + stat_r[1] + stat_r[2]
    count = 1.0 / (FEAT * ROWS)
    mean = total[:, 0:1] * count
    inv = lax.rsqrt(total[:, 1:2] * count - mean * mean + norm_epsilon)
    istd[...] = jnp.broadcast_to(inv, (OWN, 128))
    centred = (x - mean) * inv
    cen[...] = centred
    normed = (centred * gain[...].astype(f32) + shift[...].astype(f32)).astype(bf16)
    for k in range(CHUNKS):
        nrm[k, pl.ds(pl.multiple_of(STEP * c, STEP), STEP), :] = normed[STEP * k : STEP * (k + 1)]

    def token_rows(k, col):
        return nrm.at[k, pl.ds(pl.multiple_of(STEP * col, STEP), STEP)]

    def nlo_copy(k, col):
        return remote(token_rows(k, col), token_rows(k, col), nlo_sem, (k,), {"col": pc})

    def y_peer(j):
        return {"col": ((y + j) % YS) * 2 + lo}

    def nown_copy(k, j, col):
        return remote(token_rows(k, col), token_rows(k, col), nown_sem, (k, j), y_peer(j))

    def nfwd_copy(k, j, col):
        return remote(token_rows(k, col), token_rows(k, col), nfwd_sem, (k, j), y_peer(j))

    def send_own(k, carry):
        nlo_copy(k, c).start()
        for j in range(1, YS):
            nown_copy(k, j, c).start()
        return carry

    lax.fori_loop(0, CHUNKS, send_own, 0)

    def forward_tokens(k):
        nlo_copy(k, pc).wait_recv()
        for j in range(1, YS):
            nfwd_copy(k, j, pc).start()

    forward_tokens(0)

    for j in range(1, DEPTH):
        owner = (d + DEPTH - j) % DEPTH
        dng_copy(j, owner).wait_recv()
        upg_copy(j, owner).wait_recv()
    for i in range(DEPTH):
        u = upg[i]
        high = u.astype(bf16)
        mid_part = (u - high.astype(f32)).astype(bf16)
        zero = jnp.zeros_like(high)
        cols = slice(UPB * i, UPB * (i + 1))
        u_low[:, cols] = jnp.concatenate([high, high, high, zero], axis=0)
        u_prod[:, cols] = jnp.concatenate([high, mid_part, high, zero], axis=0)
    for i in range(DEPTH // 2):
        u = jnp.concatenate([dng[2 * i], dng[2 * i + 1]], axis=1)
        high = u.astype(bf16)
        mid_part = (u - high.astype(f32)).astype(bf16)
        zero = jnp.zeros_like(high)
        cols = slice(2 * DNB * i, 2 * DNB * (i + 1))
        d_low[:, cols] = jnp.concatenate([high, high, high, zero], axis=0)
        d_prod[:, cols] = jnp.concatenate([high, mid_part, high, zero], axis=0)
    up_acc[...] = jnp.zeros_like(up_acc)
    dn_acc[...] = jnp.zeros_like(dn_acc)
    w_copy.wait()
    cot_copy.wait()

    def split(value):
        high = value.astype(bf16).astype(f32)
        lanes = lax.broadcasted_iota(jnp.int32, value.shape, 1)
        return jnp.where(lanes < 2 * RANK, high, value - high).astype(bf16)

    def part_rows(k, owner, half):
        start = pl.multiple_of(RING * owner + STEP * half, STEP)
        return k, pl.ds(start, STEP)

    def rs_copy(k, slot):
        target = right if slot < 3 else left
        return remote(rs_s.at[k, slot], rs_r.at[k, slot], rs_sem, (k, slot), {"row": target})

    def rs_decoder(k, slot):
        return decoder(lambda t, n: rs_r[k, slot, :, t : t + n], HID)

    def rs_send(k, slot, owner, half):
        kk, rows = part_rows(k, owner, half)

        def store(t, n, value):
            rs_s[k, slot, :, t : t + n] = value

        encode(lambda t: part[kk, rows, t : t + TILE], store, STEP, HID)
        rs_copy(k, slot).start()

    def phase_forward(k):
        for j in range(1, YS):
            source = (y + YS - j) % YS
            nown_copy(k, j, source * 2 + lo).wait_recv()
            nfwd_copy(k, j, source * 2 + (1 - lo)).wait_recv()
        lhs = nrm[k]
        rank = split(
            adapter_scale
            * lax.dot_general(lhs, d_low[...], NT, preferred_element_type=f32)
        )
        low[k] = rank

        def tile(t, carry):
            cols = pl.ds(pl.multiple_of(t * TILE, TILE), TILE)
            part[k, :, cols] = jnp.dot(
                nrm[k], w[:, cols], preferred_element_type=f32
            ) + jnp.dot(low[k], u_prod[:, cols], preferred_element_type=f32)
            return carry

        lax.fori_loop(0, HID // TILE, tile, 0)
        rs_send(k, 0, opp, 0)
        rs_send(k, 3, opp, 1)
        rs_send(k, 1, right, 1)
        rs_send(k, 4, left, 0)

    def phase_relay(k):
        for slot, owner, half in ((0, right, 0), (3, left, 1)):
            rs_copy(k, slot).wait_recv()
            kk, rows = part_rows(k, owner, half)
            got = rs_decoder(k, slot)
            for t in range(0, HID, TILE):
                part[kk, rows, t : t + TILE] += got(t)
            rs_send(k, slot + 2, owner, half)

    def slope_rows(k, owner, first, count_):
        return slg.at[k, pl.ds(pl.multiple_of(RING * owner + first, STEP), count_)]

    def ag_copy(k, slot, owner):
        rows = (
            slope_rows(k, owner, 0, RING)
            if slot in (0, 2)
            else slope_rows(k, owner, 0 if slot == 1 else STEP, STEP)
        )
        target = right if slot < 2 else left
        return remote(rows, rows, ag_sem, (k, slot), {"row": target})

    def phase_middle(k):
        for half, first, second in ((0, 4, 2), (1, 1, 5)):
            rs_copy(k, first).wait_recv()
            rs_copy(k, second).wait_recv()
            kk, rows = part_rows(k, r, half)
            one, two = rs_decoder(k, first), rs_decoder(k, second)
            start = pl.multiple_of(OWN * half + STEP * k, STEP)
            for t in range(0, HID, TILE):
                cols = slice(t, t + TILE)
                v = part[kk, rows, cols] + one(t) + two(t) + bias[:, cols].astype(f32)
                value, slope = gelu_both(v)
                hidden[pl.ds(start, STEP), cols] = value.astype(bf16)
                slg[kk, rows, cols] = (
                    cot[pl.ds(start, STEP), cols].astype(f32) * slope
                ).astype(bf16)
        ag_copy(k, 0, r).start()
        ag_copy(k, 2, r).start()

    def phase_spread(k):
        ag_copy(k, 0, left).wait_recv()
        ag_copy(k, 1, left).start()
        ag_copy(k, 2, right).wait_recv()
        ag_copy(k, 3, right).start()

    def cs_copy(k, j):
        return remote(cs_s.at[k, j - 1], cs_r.at[k, j - 1], cs_sem, (k, j), y_peer(j))

    def phase_backward(k):
        ag_copy(k, 1, opp).wait_recv()
        ag_copy(k, 3, opp).wait_recv()
        slopes = slg[k]
        rank = split(
            adapter_scale * lax.dot_general(slopes, u_low[...], NT, preferred_element_type=f32)
        )
        bsize = 256

        def tile(t, carry):
            rows = pl.ds(pl.multiple_of(t * bsize, bsize), bsize)
            back[k, :, rows] = lax.dot_general(
                slg[k], w[rows, :], NT, preferred_element_type=f32
            ) + jnp.dot(rank, d_prod[:, rows], preferred_element_type=f32)
            return carry

        lax.fori_loop(0, FEAT // bsize, tile, 0)
        for j in range(1, YS):
            rows = pl.ds(pl.multiple_of(RING * ((y + j) % YS), RING), RING)

            def store(t, n, value):
                cs_s[k, j - 1, :, t : t + n] = value

            encode(lambda t: back[k, rows, t : t + TILE], store, RING, FEAT)
            cs_copy(k, j).start()
        low_t = low[k].astype(f32).T.astype(bf16)
        rank_t = rank.astype(f32).T.astype(bf16)

        def grow(t, carry):
            cols = pl.ds(pl.multiple_of(t * TILE, TILE), TILE)
            g = jnp.dot(low_t, slg[k, :, cols], preferred_element_type=f32)
            up_acc[:, cols] += g[0:RANK] + g[2 * RANK : 3 * RANK]
            return carry

        lax.fori_loop(0, HID // TILE, grow, 0)

        def grow_down(t, carry):
            cols = pl.ds(pl.multiple_of(t * TILE, TILE), TILE)
            g = jnp.dot(rank_t, nrm[k, :, cols], preferred_element_type=f32)
            dn_acc[:, cols] += g[0:RANK] + g[2 * RANK : 3 * RANK]
            return carry

        lax.fori_loop(0, FEAT // TILE, grow_down, 0)

    def lo_copy(k):
        return remote(lo_s.at[k], lo_r.at[k], lo_sem, (k,), {"col": pc})

    def phase_fold(k):
        mine = pl.ds(pl.multiple_of(RING * y, RING), RING)
        for j in range(1, YS):
            cs_copy(k, j).wait_recv()
            got = decoder(lambda t, n: cs_r[k, j - 1, :, t : t + n], FEAT)
            for t in range(0, FEAT, TILE):
                back[k, mine, t : t + TILE] += got(t)
        other = pl.ds(pl.multiple_of(RING * y + STEP * (1 - lo), STEP), STEP)

        def store(t, n, value):
            lo_s[k, :, t : t + n] = value

        encode(lambda t: back[k, other, t : t + TILE], store, STEP, FEAT)
        lo_copy(k).start()

    def gst_copy(k, j):
        return remote(gst_s.at[k], gst_r.at[k, j - 1], gst_sem, (k, j), {"row": (r + j) % ROWS})

    def own_rows(k):
        return pl.ds(pl.multiple_of(STEP * k, STEP), STEP)

    def phase_stats(k):
        lo_copy(k).wait_recv()
        mine = pl.ds(pl.multiple_of(RING * y + STEP * lo, STEP), STEP)
        got = decoder(lambda t, n: lo_r[k, :, t : t + n], FEAT)
        one = jnp.zeros((STEP, 1), f32)
        two = jnp.zeros((STEP, 1), f32)
        for t in range(0, FEAT, TILE):
            cols = slice(t, t + TILE)
            scaled = (back[k, mine, cols] + got(t)) * gain[:, cols].astype(f32)
            ng[k, :, cols] = scaled
            one += jnp.sum(scaled, axis=1, keepdims=True)
            two += jnp.sum(scaled * cen[own_rows(k), cols], axis=1, keepdims=True)
        lanes = lax.broadcasted_iota(jnp.int32, (STEP, 128), 1)
        gst_s[k] = jnp.where(lanes == 0, one, jnp.where(lanes == 1, two, 0.0))
        for j in range(1, ROWS):
            gst_copy(k, j).start()

    def phase_finish(k):
        for j in range(1, ROWS):
            gst_copy(k, j).wait_recv()
        sums = (gst_s[k] + gst_r[k, 0] + gst_r[k, 1] + gst_r[k, 2]) * count
        inv_ = istd[own_rows(k), 0:1]
        for t in range(0, FEAT, TILE):
            cols = slice(t, t + TILE)
            input_grad[own_rows(k), cols] = (
                inv_ * (ng[k, :, cols] - sums[:, 0:1] - cen[own_rows(k), cols] * sums[:, 1:2])
            ).astype(bf16)

    def ug_copy(j):
        peer = (d + j) % DEPTH
        return remote(ugs.at[peer], ugr.at[j], ug_sem, (j,), {"depth": peer})

    def dg_copy(j):
        peer = (d + j) % DEPTH
        return remote(dgs.at[peer], dgr.at[j], dg_sem, (j,), {"depth": peer})

    def ux_copy(j, owner):
        return remote(upx.at[owner], upx.at[owner], ux_sem, (j,), {"row": (r + j) % ROWS})

    def dx_copy(j, owner):
        return remote(dnx.at[owner], dnx.at[owner], dx_sem, (j,), {"col": (c + j) % COLS})

    def grads_send():
        for i in range(DEPTH):
            ugs[i] = up_acc[:, UPB * i : UPB * (i + 1)]
            dgs[i] = dn_acc[:, DNB * i : DNB * (i + 1)]
        for j in range(1, DEPTH):
            ug_copy(j).start()
            dg_copy(j).start()

    def grads_spread():
        up_sum = ugs[d]
        dn_sum = dgs[d]
        for j in range(1, DEPTH):
            ug_copy(j).wait_recv()
            dg_copy(j).wait_recv()
            up_sum += ugr[j]
            dn_sum += dgr[j]
        upx[r] = up_sum
        dnx[c] = dn_sum
        for j in range(1, ROWS):
            ux_copy(j, r).start()
        for j in range(1, COLS):
            dx_copy(j, c).start()

    def iteration(it, carry):
        @pl.when(it < CHUNKS)
        def _():
            phase_forward(it)

        @pl.when(it < CHUNKS - 1)
        def _():
            forward_tokens(it + 1)

        @pl.when(it < CHUNKS)
        def _():
            phase_relay(it)

        @pl.when((it >= 3) & (it < CHUNKS + 3))
        def _():
            phase_backward(it - 3)

        @pl.when(it == CHUNKS + 2)
        def _():
            grads_send()

        @pl.when((it >= 2) & (it < CHUNKS + 2))
        def _():
            phase_spread(it - 2)

        @pl.when((it >= 1) & (it < CHUNKS + 1))
        def _():
            phase_middle(it - 1)

        @pl.when((it >= 4) & (it < CHUNKS + 4))
        def _():
            phase_fold(it - 4)

        @pl.when(it == CHUNKS + 3)
        def _():
            grads_spread()

        @pl.when((it >= 5) & (it < CHUNKS + 5))
        def _():
            phase_stats(it - 5)

        @pl.when(it >= 6)
        def _():
            phase_finish(it - 6)

        return carry

    lax.fori_loop(0, CHUNKS + 6, iteration, 0)

    for j in range(1, ROWS):
        ux_copy(j, (r + ROWS - j) % ROWS).wait_recv()
    for j in range(1, COLS):
        dx_copy(j, (c + COLS - j) % COLS).wait_recv()
    up_gradient = upx[0]
    for i in range(1, ROWS):
        up_gradient += upx[i]
    down_gradient = dnx[0]
    for i in range(1, COLS):
        down_gradient += dnx[i]
    new_up_w[...], new_up_m[...], new_up_s[...] = adam(up_w[...], up_m[...], up_s[...], up_gradient)
    new_down_w[...], new_down_m[...], new_down_s[...] = adam(
        down_w[...], down_m[...], down_s[...], down_gradient
    )

    for j in range(1, ROWS):
        stat_copy(j).wait_send()
        ux_copy(j, r).wait_send()
    for j in range(1, COLS):
        dx_copy(j, c).wait_send()
    for j in range(1, DEPTH):
        dng_copy(j, d).wait_send()
        upg_copy(j, d).wait_send()
        ug_copy(j).wait_send()
        dg_copy(j).wait_send()

    def drain(k, carry):
        nlo_copy(k, c).wait_send()
        for j in range(1, YS):
            nown_copy(k, j, c).wait_send()
            nfwd_copy(k, j, pc).wait_send()
            cs_copy(k, j).wait_send()
        for slot in range(6):
            rs_copy(k, slot).wait_send()
        for slot, owner in ((0, r), (1, left), (2, r), (3, right)):
            ag_copy(k, slot, owner).wait_send()
        lo_copy(k).wait_send()
        for j in range(1, ROWS):
            gst_copy(k, j).wait_send()
        return carry

    lax.fori_loop(0, CHUNKS, drain, 0)


def shards(*blocks):
    (tok, w, bias, gain, shift, down_w, up_w, down_m, down_s, up_m, up_s, cot) = blocks
    vmem = pl.BlockSpec(memory_space=pltpu.VMEM)
    hbm = pl.BlockSpec(memory_space=pl.ANY)
    n = CHUNKS
    dma = pltpu.SemaphoreType.DMA
    small = jax.ShapeDtypeStruct((RANK, DNB), f32)
    wide = jax.ShapeDtypeStruct((RANK, UPB), f32)
    scratch = [
        pltpu.VMEM((FEAT, HID), bf16),
        pltpu.VMEM((2 * OWN, HID), bf16),
        dma((2,)),
        pltpu.VMEM((OWN, 128), f32),
        pltpu.VMEM((ROWS - 1, OWN, 128), f32),
        pltpu.VMEM((OWN, FEAT), f32),
        pltpu.VMEM((OWN, 128), f32),
        pltpu.VMEM((n, TOK, FEAT), bf16),
        pltpu.VMEM((DEPTH, RANK, UPB), f32),
        pltpu.VMEM((DEPTH, RANK, DNB), f32),
        pltpu.VMEM((4 * RANK, FEAT), bf16),
        pltpu.VMEM((4 * RANK, FEAT), bf16),
        pltpu.VMEM((4 * RANK, HID), bf16),
        pltpu.VMEM((4 * RANK, HID), bf16),
        pltpu.VMEM((n, TOK, HID), f32),
        pltpu.VMEM((n, TOK, 4 * RANK), bf16),
        pltpu.VMEM((n, 6, STEP, HID + 128), bf16),
        pltpu.VMEM((n, 6, STEP, HID + 128), bf16),
        pltpu.VMEM((n, TOK, HID), bf16),
        pltpu.VMEM((n, TOK, FEAT), f32),
        pltpu.VMEM((n, YS - 1, RING, FEAT + 128), bf16),
        pltpu.VMEM((n, YS - 1, RING, FEAT + 128), bf16),
        pltpu.VMEM((n, STEP, FEAT + 128), bf16),
        pltpu.VMEM((n, STEP, FEAT + 128), bf16),
        pltpu.VMEM((n, STEP, FEAT), f32),
        pltpu.VMEM((n, STEP, 128), f32),
        pltpu.VMEM((n, ROWS - 1, STEP, 128), f32),
        pltpu.VMEM((RANK, HID), f32),
        pltpu.VMEM((RANK, FEAT), f32),
        pltpu.VMEM((DEPTH, RANK, UPB), f32),
        pltpu.VMEM((DEPTH, RANK, UPB), f32),
        pltpu.VMEM((DEPTH, RANK, DNB), f32),
        pltpu.VMEM((DEPTH, RANK, DNB), f32),
        pltpu.VMEM((ROWS, RANK, UPB), f32),
        pltpu.VMEM((COLS, RANK, DNB), f32),
        dma((2, ROWS)),
        dma((2, n)),
        dma((2, n, YS)),
        dma((2, n, YS)),
        dma((2, DEPTH)),
        dma((2, DEPTH)),
        dma((2, n, 6)),
        dma((2, n, 4)),
        dma((2, n, YS)),
        dma((2, n)),
        dma((2, n, ROWS)),
        dma((2, DEPTH)),
        dma((2, DEPTH)),
        dma((2, ROWS)),
        dma((2, COLS)),
    ]
    return pl.pallas_call(
        kernel,
        out_shape=(
            jax.ShapeDtypeStruct((2 * OWN, HID), bf16),
            jax.ShapeDtypeStruct((OWN, FEAT), bf16),
            small,
            small,
            small,
            wide,
            wide,
            wide,
        ),
        in_specs=[vmem, hbm] + [vmem] * 9 + [hbm],
        out_specs=(vmem,) * 8,
        scratch_shapes=scratch,
        compiler_params=pltpu.CompilerParams(
            collective_id=0, has_side_effects=True, vmem_limit_bytes=56 * 1024 * 1024
        ),
        cost_estimate=pl.CostEstimate(
            flops=4 * 512 * FEAT * HID, bytes_accessed=14000000, transcendentals=10000000
        ),
        name="fused_step",
    )(
        tok,
        w,
        bias.reshape(1, HID),
        gain.reshape(1, FEAT),
        shift.reshape(1, FEAT),
        down_w,
        up_w,
        down_m,
        down_s,
        up_m,
        up_s,
        cot,
    )


def solution(mesh):
    down = P(None, ("row", "depth"))
    up = P(None, ("col", "depth"))
    return jax.shard_map(
        shards,
        mesh=mesh,
        in_specs=(
            P(("depth", "col"), "row"),
            P("row", "col"),
            P("col"),
            P("row"),
            P("row"),
            down,
            up,
            down,
            down,
            up,
            up,
            P(("depth", "row"), "col"),
        ),
        out_specs=(
            P(("depth", "row"), "col"),
            P(("depth", "col"), "row"),
            down,
            down,
            down,
            up,
            up,
            up,
        ),
        check_vma=False,
    )
```

time: 480 us -> 190 us (0.40)
  waiting for transfers between devices: 315 us -> 0 us
  Pallas kernels: 0 us -> 169 us
  blocking collectives: 96.4 us -> 0 us
  matrix products: 36.9 us -> 0 us
  between operations: 14.3 us -> 0.65 us
  other arithmetic: 12.8 us -> 0 us
  local copies, waits for them, and re-layouts: 4.02 us -> 15.9 us
    reduce_scatter x4 -> x0, waiting for transfers between devices: 205 us -> none  [the longest x1 119 us: shards(): lax.psum_scatter(main_part, 'row', scatter_dimension=0, tiled=True)]
    pallas_call x0 -> x1, Pallas kernels: none -> 169 us  [shards(): pl.pallas_call(kernel, out_shape=(jax.ShapeDtypeStruct((2 * OWN, HID), bf...]
    all_gather x2 -> x0, waiting for transfers between devices: 76.9 us -> none  [the longest x1 61.1 us: shards(): slice_slopes = lax.all_gather(activation_slopes, 'row', axis=0, tiled=True)]
    psum x3 -> x0, blocking collectives: 70 us -> none  [the longest x1 33.6 us: shards(): down_gradient = lax.psum(down_depth, 'col')]
    dot_general x8 -> x0, matrix products: 36.9 us -> none  [the longest x1 7.65 us: shards(): lax.dot_general(slice_slopes, projection_weight, (((1,), (1,)), ((), ()))...]
    unnamed x8 -> x0, waiting for transfers between devices: 33.1 us -> none
    all_gather x2 -> x0, blocking collectives: 26.4 us -> none  [the longest x1 13.4 us: shards(): lax.all_gather(adapter_down_weight, 'depth', axis=1, tiled=True)]
    convert_element_type x6 -> x0, other arithmetic: 9.13 us -> none  [the longest x1 4.12 us: shards(): (cotangent.astype(jnp.float32) * gelu_slope(preactivation_value)).astype(...]
  transfers between devices with their start and end apart: 7 -> 0, of which waited for: 7 -> 0; matrix products, arithmetic and copies ran while one was open for 5% -> 0% of each run, Pallas kernels for 0% -> 0%
where the time goes in v1:
time: 190 us; the launch traced here: 186 us
  Pallas kernels  169 us (89%)
  local copies, waits for them, and re-layouts  15.9 us (8%)
    pallas_call x1, Pallas kernels, shards(): pl.pallas_call(kernel, out_shape=(jax.ShapeDtypeStruct((2 * OWN, HID), bf...  169 us
    unnamed x8, local copies, waits for them, and re-layouts  12.1 us

profile of v1, /device:TPU:8, one launch (start us, length us, event | category | flops | bytes accessed | tf_op | source)
XLA Modules:
  0.0 186.0 jit_solution(8185855582779676648)
XLA Ops:
  0.6 1.3 reshape.26.gain
  1.9 1.3 reshape.27.shift
  3.2 1.3 reshape.25.bias
  4.5 169.5 %fused_step.1 = (bf16[128,3072]{1,0:T(8,128)(2,1)}, bf16[64,1536]{1,0:T(8,128)(2,1)}, f32[32,192]{1,0:T(8,128)}, f32[32,192]{1,0:T(8,128)}, f32[32,192]{1,0:T(8,...) custom-call(bf16[64,1536]{1,0:T(8,128)(2,1)} %tok.1, bf16[1536,3072]{1,0:T(8,128)(2,1)} %w_hbm.1, ...), custom_call_target="tpu_custom_call" | custom-call | flops 9663676416 | bytes 14000000 | tf_op jit(solution)/shard_map/fused_step/pallas_call | solution.py:653
  174.0 2.1 %copy.28 = bf16[128,3072]{1,0:T(8,128)(2,1)} copy(bf16[128,3072]{1,0:T(8,128)(2,1)} %get-tuple-element.16) | data formatting | bytes 1572864
  176.0 1.6 copy.29
  177.7 1.4 copy.30
  179.0 1.4 copy.31
  180.4 1.4 copy.32
  181.8 1.4 copy.33
  183.2 1.4 copy.34
  184.6 1.4 copy.35

commit v2 on v1

v2 whole, which is shorter than its diff:
```python
import functools
import jax
import jax.numpy as jnp
from jax import lax
from jax.experimental import pallas as pl
from jax.experimental.pallas import tpu as pltpu
from jax.sharding import PartitionSpec as P

adapter_scale = 0.5
norm_epsilon = 1e-05
beta_first = 0.9
beta_second = 0.999
adam_step = 10
learn_rate = 0.01
decay_rate = 0.1
adam_epsilon = 1e-08

f32 = jnp.float32
bf16 = jnp.bfloat16
MESH = pl.DeviceIdType.MESH
NT = (((1,), (1,)), ((), ()))

ROWS, COLS, DEPTH = 4, 8, 8
YS = COLS // 2
CHUNKS = 4
OWN = 64
STEP = OWN // CHUNKS
TOK = STEP * COLS
FEAT, HID, RANK = 1536, 3072, 32
UPB, DNB = HID // DEPTH, FEAT // DEPTH
RING = 2 * STEP
CODE_SPAN = 120.0
LN2 = 0.6931471805599453
TILE = 512


def gelu_both(v):
    inner = 0.7978845608 * (v + 0.044715 * v * v * v)
    tangent = jnp.tanh(inner)
    value = 0.5 * v * (1.0 + tangent)
    slope = 0.5 * (1.0 + tangent) + 0.5 * v * (1.0 - tangent * tangent) * 0.7978845608 * (
        1.0 + 3.0 * 0.044715 * v * v
    )
    return value, slope


def adam(weight, moment, square, gradient):
    new_moment = beta_first * moment + (1.0 - beta_first) * gradient
    new_square = beta_second * square + (1.0 - beta_second) * gradient * gradient
    update = (
        new_moment
        / (1.0 - beta_first**adam_step)
        / (jnp.sqrt(new_square / (1.0 - beta_second**adam_step)) + adam_epsilon)
    )
    return weight - learn_rate * (update + decay_rate * weight), new_moment, new_square


def encode(load, store, rows, width):
    top = jnp.zeros((rows, 1), f32)
    for t in range(0, width, TILE):
        top = jnp.maximum(top, jnp.max(jnp.abs(load(t)), axis=1, keepdims=True))
    top = (jnp.maximum(top, 1e-30) * 1.01).astype(bf16)
    factor = CODE_SPAN / top.astype(f32)
    for t in range(0, width, TILE):
        store(t, TILE, jnp.exp2(load(t) * factor).astype(bf16))
    store(width, 128, jnp.broadcast_to(top, (rows, 128)))


def decoder(load, width):
    scale = load(width, 128)[:, 0:1].astype(f32) * (1.0 / (CODE_SPAN * LN2))
    return lambda t: jnp.log(load(t, TILE).astype(f32)) * scale


def kernel(
    tok,
    w_hbm,
    bias,
    gain,
    shift,
    down_w,
    up_w,
    cot_hbm,
    hidden,
    input_grad,
    down_grad,
    up_grad,
    w,
    cot,
    local_sem,
    stat_s,
    stat_r,
    gain_row,
    shift_row,
    bias_row,
    raw,
    mst,
    nrm,
    upg,
    dng,
    d_low,
    d_prod,
    u_low,
    u_prod,
    part,
    low,
    rs_s,
    rs_r,
    slg,
    back,
    cs_s,
    cs_r,
    lo_s,
    lo_r,
    ng,
    gst_s,
    gst_r,
    low_own,
    dn_acc,
    ugs,
    ugr,
    dgs,
    dgr,
    upx,
    dnx,
    stat_sem,
    mst_sem,
    nlo_sem,
    nown_sem,
    nfwd_sem,
    upg_sem,
    dng_sem,
    rs_sem,
    ag_sem,
    cs_sem,
    lo_sem,
    gst_sem,
    ug_sem,
    dg_sem,
    ux_sem,
    dx_sem,
):
    r = lax.axis_index("row")
    c = lax.axis_index("col")
    d = lax.axis_index("depth")
    y, lo = c // 2, c % 2
    right, left, opp = (r + 1) % ROWS, (r + 3) % ROWS, (r + 2) % ROWS
    pc = y * 2 + (1 - lo)

    def remote(src, dst, sems, index, device):
        return pltpu.make_async_remote_copy(
            src_ref=src,
            dst_ref=dst,
            send_sem=sems.at[(0,) + index],
            recv_sem=sems.at[(1,) + index],
            device_id=device,
            device_id_type=MESH,
        )

    w_copy = pltpu.make_async_copy(w_hbm, w, local_sem.at[0])
    cot_copy = pltpu.make_async_copy(cot_hbm, cot, local_sem.at[1])
    w_copy.start()
    cot_copy.start()

    barrier = pltpu.get_barrier_semaphore()
    for j in range(1, ROWS):
        pl.semaphore_signal(barrier, inc=1, device_id={"row": (r + j) % ROWS}, device_id_type=MESH)
    for j in range(1, COLS):
        pl.semaphore_signal(barrier, inc=1, device_id={"col": (c + j) % COLS}, device_id_type=MESH)
    for j in range(1, DEPTH):
        pl.semaphore_signal(
            barrier, inc=1, device_id={"depth": (d + j) % DEPTH}, device_id_type=MESH
        )

    x = tok[...].astype(f32)
    lane = lax.broadcasted_iota(jnp.int32, (OWN, 128), 1)
    s1 = jnp.sum(x, axis=1, keepdims=True)
    s2 = jnp.sum(x * x, axis=1, keepdims=True)
    sums = jnp.where(lane == 0, s1, jnp.where(lane == 1, s2, 0.0))
    stat_s[...] = jnp.concatenate([sums, jnp.zeros_like(sums)], axis=0).T[0:8]
    upg[d] = up_w[...]
    dng[d] = down_w[...]
    for k in range(CHUNKS):
        raw[k, pl.ds(pl.multiple_of(STEP * c, STEP), STEP), :] = tok[STEP * k : STEP * (k + 1), :]
    pl.semaphore_wait(barrier, ROWS + COLS + DEPTH - 3)

    def stat_copy(j):
        return remote(stat_s, stat_r.at[j - 1], stat_sem, (j,), {"row": (r + j) % ROWS})

    def upg_copy(j, owner):
        return remote(upg.at[owner], upg.at[owner], upg_sem, (j,), {"depth": (d + j) % DEPTH})

    def dng_copy(j, owner):
        return remote(dng.at[owner], dng.at[owner], dng_sem, (j,), {"depth": (d + j) % DEPTH})

    for j in range(1, ROWS):
        stat_copy(j).start()

    def token_rows(k, col):
        return raw.at[k, pl.ds(pl.multiple_of(STEP * col, STEP), STEP)]

    def nlo_copy(k, col):
        return remote(token_rows(k, col), token_rows(k, col), nlo_sem, (k,), {"col": pc})

    def y_peer(j):
        return {"col": ((y + j) % YS) * 2 + lo}

    def nown_copy(k, j, col):
        return remote(token_rows(k, col), token_rows(k, col), nown_sem, (k, j), y_peer(j))

    def nfwd_copy(k, j, col):
        return remote(token_rows(k, col), token_rows(k, col), nfwd_sem, (k, j), y_peer(j))

    def ndiag_copy(j):
        peer = {"col": ((y + j) % YS) * 2 + (1 - lo)}
        return remote(token_rows(0, c), token_rows(0, c), nfwd_sem, (0, j), peer)

    for j in range(1, YS):
        ndiag_copy(j).start()
        nown_copy(0, j, c).start()

    nlo_copy(0, c).start()
    for j in range(1, DEPTH):
        dng_copy(j, d).start()
    for j in range(1, DEPTH):
        upg_copy(j, d).start()

    def forward_tokens(k):
        nlo_copy(k, pc).wait_recv()
        for j in range(1, YS):
            nfwd_copy(k, j, pc).start()

    gain_row[...] = gain[...].astype(f32).reshape(1, FEAT)
    shift_row[...] = shift[...].astype(f32).reshape(1, FEAT)
    bias_row[...] = bias[...].astype(f32).reshape(1, HID)
    for j in range(1, ROWS):
        stat_copy(j).wait_recv()
    total = stat_s[...] + stat_r[0] + stat_r[1] + stat_r[2]
    total = jnp.concatenate([total, jnp.zeros((120, 128), f32)], axis=0).T[0:OWN]
    count = 1.0 / (FEAT * ROWS)
    mean = total[:, 0:1] * count
    inv = lax.rsqrt(total[:, 1:2] * count - mean * mean + norm_epsilon)
    both = jnp.where(lane == 0, mean, inv)
    for k in range(CHUNKS):
        mst[k, pl.ds(pl.multiple_of(STEP * c, STEP), STEP), :] = both[STEP * k : STEP * (k + 1)]

    def mst_copy(late, j, col):
        rows = pl.ds(pl.multiple_of(STEP * col, STEP), STEP)
        ref = mst.at[pl.ds(1, CHUNKS - 1), rows] if late else mst.at[0, rows]
        return remote(ref, ref, mst_sem, (late, j), {"col": (c + j) % COLS})

    for late in (0, 1):
        for j in range(1, COLS):
            mst_copy(late, j, c).start()

    def send_own(k, carry):
        nlo_copy(k, c).start()
        for j in range(1, YS):
            nown_copy(k, j, c).start()
        return carry

    lax.fori_loop(1, CHUNKS, send_own, 0)

    def adapter_operands():
        for j in range(1, DEPTH):
            dng_copy(j, (d + DEPTH - j) % DEPTH).wait_recv()
        for i in range(DEPTH // 2):
            u = jnp.concatenate([dng[2 * i], dng[2 * i + 1]], axis=1)
            high = u.astype(bf16)
            mid_part = (u - high.astype(f32)).astype(bf16)
            zero = jnp.zeros_like(high)
            cols = slice(2 * DNB * i, 2 * DNB * (i + 1))
            d_low[:, cols] = jnp.concatenate([high, high, high, zero], axis=0)
            d_prod[:, cols] = jnp.concatenate([high, mid_part, high, zero], axis=0)
        for j in range(1, DEPTH):
            upg_copy(j, (d + DEPTH - j) % DEPTH).wait_recv()
        for i in range(DEPTH):
            u = upg[i]
            high = u.astype(bf16)
            mid_part = (u - high.astype(f32)).astype(bf16)
            zero = jnp.zeros_like(high)
            cols = slice(UPB * i, UPB * (i + 1))
            u_low[:, cols] = jnp.concatenate([high, high, high, zero], axis=0)
            u_prod[:, cols] = jnp.concatenate([high, mid_part, high, zero], axis=0)

    dn_acc[...] = jnp.zeros_like(dn_acc)
    w_copy.wait()
    cot_copy.wait()

    def split(value):
        high = value.astype(bf16).astype(f32)
        lanes = lax.broadcasted_iota(jnp.int32, value.shape, 1)
        return jnp.where(lanes < 2 * RANK, high, value - high).astype(bf16)

    def part_rows(k, owner, half):
        start = pl.multiple_of(RING * owner + STEP * half, STEP)
        return k, pl.ds(start, STEP)

    def rs_copy(k, slot):
        target = right if slot < 3 else left
        return remote(rs_s.at[k, slot], rs_r.at[k, slot], rs_sem, (k, slot), {"row": target})

    tail = lax.broadcasted_iota(jnp.int32, (STEP, 128), 1)

    def rs_decoder(k, slot):
        last = rs_r[k, slot, :, HID : HID + 128].astype(f32) * 1.0
        main = decoder(
            lambda t, n: last[:, 64:128] if t == HID else rs_r[k, slot, :, t : t + n], HID
        )
        scale = last[:, 96:97] * (1.0 / (CODE_SPAN * LN2))
        return main, jnp.where(tail < 2 * RANK, jnp.log(last) * scale, 0.0)

    def rs_send(k, slot, owner, half):
        kk, rows = part_rows(k, owner, half)
        value = part[kk, rows, HID : HID + 128]
        top = jnp.max(jnp.abs(value), axis=1, keepdims=True)
        top = (jnp.maximum(top, 1e-30) * 1.01).astype(bf16).astype(f32)
        code = jnp.exp2(value * (CODE_SPAN / top))

        def store(t, n, coded):
            if t == HID:
                scale = jnp.where(tail < 3 * RANK, coded.astype(f32), top)
                coded = jnp.where(tail < 2 * RANK, code, scale).astype(bf16)
            rs_s[k, slot, :, t : t + n] = coded

        encode(lambda t: part[kk, rows, t : t + TILE], store, STEP, HID)
        rs_copy(k, slot).start()

    def phase_forward(k):
        @pl.when(k == 0)
        def _():
            nlo_copy(0, pc).wait_recv()
            for j in range(1, COLS):
                mst_copy(0, j, (c + COLS - j) % COLS).wait_recv()

        @pl.when(k == 1)
        def _():
            for j in range(1, COLS):
                mst_copy(1, j, (c + COLS - j) % COLS).wait_recv()

        for j in range(1, YS):
            source = (y + YS - j) % YS
            nown_copy(k, j, source * 2 + lo).wait_recv()
            nfwd_copy(k, j, source * 2 + (1 - lo)).wait_recv()
        mean_, inv_ = mst[k, :, 0:1], mst[k, :, 1:2]
        for t in range(0, FEAT, TILE):
            cols = slice(t, t + TILE)
            nrm[k, :, cols] = (
                (raw[k, :, cols].astype(f32) - mean_) * inv_ * gain_row[:, cols]
                + shift_row[:, cols]
            ).astype(bf16)
        def rank_product():
            value = adapter_scale * lax.dot_general(
                nrm[k], d_low[...], NT, preferred_element_type=f32
            )
            part[k, :, HID : HID + 128] = value
            low[k] = split(value)

        def rank_tile(cols):
            return jnp.dot(low[k], u_prod[:, cols], preferred_element_type=f32)

        def columns(t):
            return pl.ds(pl.multiple_of(t * TILE, TILE), TILE)

        def main_tile(cols):
            return jnp.dot(nrm[k], w[:, cols], preferred_element_type=f32)

        @pl.when(k == 0)
        def _():
            def tile(t, carry):
                part[k, :, columns(t)] = main_tile(columns(t))
                return carry

            def add(t, carry):
                part[k, :, columns(t)] += rank_tile(columns(t))
                return carry

            lax.fori_loop(0, HID // TILE, tile, 0)
            adapter_operands()
            rank_product()
            lax.fori_loop(0, HID // TILE, add, 0)

        @pl.when(k > 0)
        def _():
            def tile(t, carry):
                part[k, :, columns(t)] = main_tile(columns(t)) + rank_tile(columns(t))
                return carry

            rank_product()
            lax.fori_loop(0, HID // TILE, tile, 0)

        rs_send(k, 0, opp, 0)
        rs_send(k, 3, opp, 1)
        rs_send(k, 1, right, 1)
        rs_send(k, 4, left, 0)

    def phase_relay(k):
        for slot, owner, half in ((0, right, 0), (3, left, 1)):
            rs_copy(k, slot).wait_recv()
            kk, rows = part_rows(k, owner, half)
            got, low_got = rs_decoder(k, slot)
            part[kk, rows, HID : HID + 128] += low_got
            for t in range(0, HID, TILE):
                part[kk, rows, t : t + TILE] += got(t)
            rs_send(k, slot + 2, owner, half)

    def slope_rows(k, owner, first, count_):
        return slg.at[k, pl.ds(pl.multiple_of(RING * owner + first, STEP), count_)]

    ag_half = (0, 1, 0, 1, 0, 1)

    def ag_copy(k, slot, owner):
        rows = slope_rows(k, owner, STEP * ag_half[slot], STEP)
        target = right if slot < 3 else left
        return remote(rows, rows, ag_sem, (k, slot), {"row": target})

    def phase_middle(k):
        for half, first, second in ((0, 4, 2), (1, 1, 5)):
            rs_copy(k, first).wait_recv()
            rs_copy(k, second).wait_recv()
            kk, rows = part_rows(k, r, half)
            (one, low_one), (two, low_two) = rs_decoder(k, first), rs_decoder(k, second)
            low_own[k, STEP * half : STEP * (half + 1), :] = (
                part[kk, rows, HID : HID + 128] + low_one + low_two
            )
            start = pl.multiple_of(OWN * half + STEP * k, STEP)
            for t in range(0, HID, TILE):
                cols = slice(t, t + TILE)
                v = part[kk, rows, cols] + one(t) + two(t) + bias_row[:, cols]
                value, slope = gelu_both(v)
                hidden[pl.ds(start, STEP), cols] = value.astype(bf16)
                slg[kk, rows, cols] = (
                    cot[pl.ds(start, STEP), cols].astype(f32) * slope
                ).astype(bf16)
            for slot in (0,) if half == 0 else (3, 1, 4):
                ag_copy(k, slot, r).start()

    def phase_spread(k):
        ag_copy(k, 0, left).wait_recv()
        ag_copy(k, 2, left).start()
        ag_copy(k, 3, right).wait_recv()
        ag_copy(k, 5, right).start()

    def cs_copy(k, j):
        return remote(cs_s.at[k, j - 1], cs_r.at[k, j - 1], cs_sem, (k, j), y_peer(j))

    def ug_copy(j):
        peer = (d + j) % DEPTH
        return remote(ugs.at[peer], ugr.at[j], ug_sem, (j,), {"depth": peer})

    def dg_copy(j):
        peer = (d + j) % DEPTH
        return remote(dgs.at[peer], dgr.at[j], dg_sem, (j,), {"depth": peer})

    def ux_copy(j, owner):
        return remote(upx.at[owner], upx.at[owner], ux_sem, (j,), {"row": (r + j) % ROWS})

    def dx_copy(j, owner):
        return remote(dnx.at[owner], dnx.at[owner], dx_sem, (j,), {"col": (c + j) % COLS})

    def down_send():
        for i in range(DEPTH):
            dgs[i] = dn_acc[:, DNB * i : DNB * (i + 1)]
        for j in range(1, DEPTH):
            dg_copy(j).start()

    def up_send():
        lanes = lax.broadcasted_iota(jnp.int32, (RING, 128), 1)
        sides = []
        for k in range(CHUNKS):
            value = low_own[k]
            high = value.astype(bf16).astype(f32)
            both_parts = jnp.where(
                lanes < RANK, high, jnp.where(lanes < 2 * RANK, value - high, 0.0)
            )
            sides.append(both_parts.T.astype(bf16))
        for i in range(DEPTH):
            cols = slice(UPB * i, UPB * (i + 1))
            g = jnp.zeros((128, UPB), f32)
            for k in range(CHUNKS):
                rows = pl.ds(pl.multiple_of(RING * r, RING), RING)
                g += jnp.dot(sides[k], slg[k, rows, cols], preferred_element_type=f32)
            ugs[i] = g[0:RANK] + g[RANK : 2 * RANK]
        for j in range(1, DEPTH):
            ug_copy(j).start()

    def phase_backward(k):
        ag_copy(k, 1, left).wait_recv()
        ag_copy(k, 4, right).wait_recv()
        ag_copy(k, 2, opp).wait_recv()
        ag_copy(k, 5, opp).wait_recv()
        slopes = slg[k]
        rank = split(
            adapter_scale * lax.dot_general(slopes, u_low[...], NT, preferred_element_type=f32)
        )
        rank_t = rank.astype(f32).T.astype(bf16)

        def grow_down(t, carry):
            cols = pl.ds(pl.multiple_of(t * TILE, TILE), TILE)
            g = jnp.dot(rank_t, nrm[k, :, cols], preferred_element_type=f32)
            dn_acc[:, cols] += g[0:RANK] + g[2 * RANK : 3 * RANK]
            return carry

        lax.fori_loop(0, FEAT // TILE, grow_down, 0)

        @pl.when(k == CHUNKS - 1)
        def _():
            down_send()

        bsize = 256

        def tile(t, carry):
            rows = pl.ds(pl.multiple_of(t * bsize, bsize), bsize)
            back[k, :, rows] = lax.dot_general(
                slg[k], w[rows, :], NT, preferred_element_type=f32
            ) + jnp.dot(rank, d_prod[:, rows], preferred_element_type=f32)
            return carry

        lax.fori_loop(0, FEAT // bsize, tile, 0)
        for j in range(1, YS):
            rows = pl.ds(pl.multiple_of(RING * ((y + j) % YS), RING), RING)

            def store(t, n, value):
                cs_s[k, j - 1, :, t : t + n] = value

            encode(lambda t: back[k, rows, t : t + TILE], store, RING, FEAT)
            cs_copy(k, j).start()

    def lo_copy(k):
        return remote(lo_s.at[k], lo_r.at[k], lo_sem, (k,), {"col": pc})

    def phase_fold(k):
        mine = pl.ds(pl.multiple_of(RING * y, RING), RING)
        for j in range(1, YS):
            cs_copy(k, j).wait_recv()
            got = decoder(lambda t, n: cs_r[k, j - 1, :, t : t + n], FEAT)
            for t in range(0, FEAT, TILE):
                back[k, mine, t : t + TILE] += got(t)
        other = pl.ds(pl.multiple_of(RING * y + STEP * (1 - lo), STEP), STEP)

        def store(t, n, value):
            lo_s[k, :, t : t + n] = value

        encode(lambda t: back[k, other, t : t + TILE], store, STEP, FEAT)
        lo_copy(k).start()

    def gst_copy(k, j):
        return remote(gst_s.at[k], gst_r.at[k, j - 1], gst_sem, (k, j), {"row": (r + j) % ROWS})

    def own_rows(k):
        return pl.ds(pl.multiple_of(STEP * k, STEP), STEP)

    def own_centred(k, cols):
        rows = pl.ds(pl.multiple_of(STEP * c, STEP), STEP)
        return (tok[own_rows(k), cols].astype(f32) - mst[k, rows, 0:1]) * mst[k, rows, 1:2]

    def phase_stats(k):
        lo_copy(k).wait_recv()
        mine = pl.ds(pl.multiple_of(RING * y + STEP * lo, STEP), STEP)
        got = decoder(lambda t, n: lo_r[k, :, t : t + n], FEAT)
        one = jnp.zeros((STEP, 1), f32)
        two = jnp.zeros((STEP, 1), f32)
        for t in range(0, FEAT, TILE):
            cols = slice(t, t + TILE)
            scaled = (back[k, mine, cols] + got(t)) * gain_row[:, cols]
            ng[k, :, cols] = scaled
            one += jnp.sum(scaled, axis=1, keepdims=True)
            two += jnp.sum(scaled * own_centred(k, cols), axis=1, keepdims=True)
        lanes = lax.broadcasted_iota(jnp.int32, (STEP, 128), 1)
        gst_s[k] = jnp.where(lanes == 0, one, jnp.where(lanes == 1, two, 0.0))
        for j in range(1, ROWS):
            gst_copy(k, j).start()

    def phase_finish(k):
        for j in range(1, ROWS):
            gst_copy(k, j).wait_recv()
        sums = (gst_s[k] + gst_r[k, 0] + gst_r[k, 1] + gst_r[k, 2]) * count
        inv_ = mst[k, pl.ds(pl.multiple_of(STEP * c, STEP), STEP), 1:2]
        for t in range(0, FEAT, TILE):
            cols = slice(t, t + TILE)
            input_grad[own_rows(k), cols] = (
                inv_ * (ng[k, :, cols] - sums[:, 0:1] - own_centred(k, cols) * sums[:, 1:2])
            ).astype(bf16)

    def grads_spread():
        up_sum = ugs[d]
        dn_sum = dgs[d]
        for j in range(1, DEPTH):
            ug_copy(j).wait_recv()
            dg_copy(j).wait_recv()
            up_sum += ugr[j]
            dn_sum += dgr[j]
        upx[r] = up_sum
        dnx[c] = dn_sum
        for j in range(1, ROWS):
            ux_copy(j, r).start()
        for j in range(1, COLS):
            dx_copy(j, c).start()

    def drain_early():
        for j in range(1, ROWS):
            stat_copy(j).wait_send()
        for j in range(1, COLS):
            mst_copy(0, j, c).wait_send()
            mst_copy(1, j, c).wait_send()
        for j in range(1, DEPTH):
            dng_copy(j, d).wait_send()
            upg_copy(j, d).wait_send()
        for j in range(1, YS):
            ndiag_copy(j).wait_send()

        def drain_tokens(k, carry):
            for j in range(1, YS):
                nfwd_copy(k, j, pc).wait_send()
            return carry

        def drain(k, carry):
            nlo_copy(k, c).wait_send()
            for j in range(1, YS):
                nown_copy(k, j, c).wait_send()
            for slot in range(6):
                rs_copy(k, slot).wait_send()
            return carry

        lax.fori_loop(0, CHUNKS, drain, 0)
        lax.fori_loop(1, CHUNKS, drain_tokens, 0)

    def iteration(it, carry):
        def step(condition, run):
            pl.when(condition)(run)

        step(it < CHUNKS, lambda: phase_forward(it))

        @pl.when(it == 0)
        def _():
            for k in range(1, CHUNKS):
                forward_tokens(k)

        step((it >= 2) & (it < CHUNKS), lambda: phase_spread(it - 2))
        step(it < CHUNKS, lambda: phase_relay(it))
        step((it >= 1) & (it < CHUNKS + 1), lambda: phase_middle(it - 1))
        step((it >= CHUNKS) & (it < CHUNKS + 2), lambda: phase_spread(it - 2))
        step(it == CHUNKS, up_send)
        step(it == CHUNKS + 2, drain_early)
        step((it >= 3) & (it < CHUNKS + 3), lambda: phase_backward(it - 3))
        step(it == CHUNKS + 2, grads_spread)
        step(it >= CHUNKS + 2, lambda: phase_finish(it - CHUNKS - 2))
        step((it >= CHUNKS + 1) & (it < CHUNKS * 2 + 1), lambda: phase_stats(it - CHUNKS - 1))
        step((it >= CHUNKS) & (it < CHUNKS * 2), lambda: phase_fold(it - CHUNKS))
        return carry

    lax.fori_loop(0, CHUNKS * 2 + 2, iteration, 0)

    for j in range(1, ROWS):
        ux_copy(j, (r + ROWS - j) % ROWS).wait_recv()
    for j in range(1, COLS):
        dx_copy(j, (c + COLS - j) % COLS).wait_recv()
    up_gradient = upx[0]
    for i in range(1, ROWS):
        up_gradient += upx[i]
    down_gradient = dnx[0]
    for i in range(1, COLS):
        down_gradient += dnx[i]
    up_grad[...] = up_gradient
    down_grad[...] = down_gradient

    for j in range(1, ROWS):
        ux_copy(j, r).wait_send()
    for j in range(1, COLS):
        dx_copy(j, c).wait_send()
    for j in range(1, DEPTH):
        ug_copy(j).wait_send()
        dg_copy(j).wait_send()

    def drain(k, carry):
        for j in range(1, YS):
            cs_copy(k, j).wait_send()
        for slot, owner in ((0, r), (1, r), (2, left), (3, r), (4, r), (5, right)):
            ag_copy(k, slot, owner).wait_send()
        lo_copy(k).wait_send()
        for j in range(1, ROWS):
            gst_copy(k, j).wait_send()
        return carry

    lax.fori_loop(0, CHUNKS, drain, 0)


def update_kernel(
    hidden,
    input_grad,
    down_grad,
    up_grad,
    down_w,
    up_w,
    down_m,
    down_s,
    up_m,
    up_s,
    hidden_out,
    input_grad_out,
    new_down_w,
    new_down_m,
    new_down_s,
    new_up_w,
    new_up_m,
    new_up_s,
    sems,
):
    copies = (
        pltpu.make_async_copy(hidden, hidden_out, sems.at[0]),
        pltpu.make_async_copy(input_grad, input_grad_out, sems.at[1]),
    )
    for copy in copies:
        copy.start()
    new_up_w[...], new_up_m[...], new_up_s[...] = adam(
        up_w[...], up_m[...], up_s[...], up_grad[...]
    )
    new_down_w[...], new_down_m[...], new_down_s[...] = adam(
        down_w[...], down_m[...], down_s[...], down_grad[...]
    )
    for copy in copies:
        copy.wait()


def shards(*blocks):
    (tok, w, bias, gain, shift, down_w, up_w, down_m, down_s, up_m, up_s, cot) = blocks
    vmem = pl.BlockSpec(memory_space=pltpu.VMEM)
    hbm = pl.BlockSpec(memory_space=pl.ANY)
    n = CHUNKS
    dma = pltpu.SemaphoreType.DMA
    small = jax.ShapeDtypeStruct((RANK, DNB), f32)
    wide = jax.ShapeDtypeStruct((RANK, UPB), f32)
    scratch = [
        pltpu.VMEM((FEAT, HID), bf16),
        pltpu.VMEM((2 * OWN, HID), bf16),
        dma((2,)),
        pltpu.VMEM((8, 128), f32),
        pltpu.VMEM((ROWS - 1, 8, 128), f32),
        pltpu.VMEM((1, FEAT), f32),
        pltpu.VMEM((1, FEAT), f32),
        pltpu.VMEM((1, HID), f32),
        pltpu.VMEM((n, TOK, FEAT), bf16),
        pltpu.VMEM((n, TOK, 128), f32),
        pltpu.VMEM((n, TOK, FEAT), bf16),
        pltpu.VMEM((DEPTH, RANK, UPB), f32),
        pltpu.VMEM((DEPTH, RANK, DNB), f32),
        pltpu.VMEM((4 * RANK, FEAT), bf16),
        pltpu.VMEM((4 * RANK, FEAT), bf16),
        pltpu.VMEM((4 * RANK, HID), bf16),
        pltpu.VMEM((4 * RANK, HID), bf16),
        pltpu.VMEM((n, TOK, HID + 128), f32),
        pltpu.VMEM((n, TOK, 4 * RANK), bf16),
        pltpu.VMEM((n, 6, STEP, HID + 128), bf16),
        pltpu.VMEM((n, 6, STEP, HID + 128), bf16),
        pltpu.VMEM((n, TOK, HID), bf16),
        pltpu.VMEM((n, TOK, FEAT), f32),
        pltpu.VMEM((n, YS - 1, RING, FEAT + 128), bf16),
        pltpu.VMEM((n, YS - 1, RING, FEAT + 128), bf16),
        pltpu.VMEM((n, STEP, FEAT + 128), bf16),
        pltpu.VMEM((n, STEP, FEAT + 128), bf16),
        pltpu.VMEM((n, STEP, FEAT), f32),
        pltpu.VMEM((n, STEP, 128), f32),
        pltpu.VMEM((n, ROWS - 1, STEP, 128), f32),
        pltpu.VMEM((n, RING, 128), f32),
        pltpu.VMEM((RANK, FEAT), f32),
        pltpu.VMEM((DEPTH, RANK, UPB), f32),
        pltpu.VMEM((DEPTH, RANK, UPB), f32),
        pltpu.VMEM((DEPTH, RANK, DNB), f32),
        pltpu.VMEM((DEPTH, RANK, DNB), f32),
        pltpu.VMEM((ROWS, RANK, UPB), f32),
        pltpu.VMEM((COLS, RANK, DNB), f32),
        dma((2, ROWS)),
        dma((2, 2, COLS)),
        dma((2, n)),
        dma((2, n, YS)),
        dma((2, n, YS)),
        dma((2, DEPTH)),
        dma((2, DEPTH)),
        dma((2, n, 6)),
        dma((2, n, 6)),
        dma((2, n, YS)),
        dma((2, n)),
        dma((2, n, ROWS)),
        dma((2, DEPTH)),
        dma((2, DEPTH)),
        dma((2, ROWS)),
        dma((2, COLS)),
    ]
    outs = pl.pallas_call(
        kernel,
        out_shape=(
            jax.ShapeDtypeStruct((2 * OWN, HID), bf16),
            jax.ShapeDtypeStruct((OWN, FEAT), bf16),
            small,
            wide,
        ),
        in_specs=[vmem, hbm] + [vmem] * 5 + [hbm],
        out_specs=(vmem,) * 4,
        scratch_shapes=scratch,
        compiler_params=pltpu.CompilerParams(
            collective_id=0, has_side_effects=True, vmem_limit_bytes=56 * 1024 * 1024
        ),
        cost_estimate=pl.CostEstimate(
            flops=4 * 512 * FEAT * HID, bytes_accessed=14000000, transcendentals=10000000
        ),
        name="fused_step",
    )(tok, w, bias, gain, shift, down_w, up_w, cot)
    return pl.pallas_call(
        update_kernel,
        out_shape=(
            jax.ShapeDtypeStruct((2 * OWN, HID), bf16),
            jax.ShapeDtypeStruct((OWN, FEAT), bf16),
            small,
            small,
            small,
            wide,
            wide,
            wide,
        ),
        in_specs=[vmem] * 10,
        out_specs=(hbm, hbm) + (vmem,) * 6,
        scratch_shapes=[dma((2,))],
        name="adapter_update",
    )(*outs, down_w, up_w, down_m, down_s, up_m, up_s)


def solution(mesh):
    down = P(None, ("row", "depth"))
    up = P(None, ("col", "depth"))
    return jax.shard_map(
        shards,
        mesh=mesh,
        in_specs=(
            P(("depth", "col"), "row"),
            P("row", "col"),
            P("col"),
            P("row"),
            P("row"),
            down,
            up,
            down,
            down,
            up,
            up,
            P(("depth", "row"), "col"),
        ),
        out_specs=(
            P(("depth", "row"), "col"),
            P(("depth", "col"), "row"),
            down,
            down,
            down,
            up,
            up,
            up,
        ),
        check_vma=False,
    )
```

time: 190 us -> 167 us (0.88); the launches traced: 186 us -> 167 us
  local copies, waits for them, and re-layouts: 15.9 us -> 0 us
  Pallas kernels: 169 us -> 166 us
    unnamed x8 -> x0, local copies, waits for them, and re-layouts: 12.1 us -> none
    pallas_call x1, Pallas kernels: 169 us -> 163 us  [shards(): pl.pallas_call(kernel, out_shape=(jax.ShapeDtypeStruct((2 * OWN, HID), bf...]
    reshape x3 -> x0, local copies, waits for them, and re-layouts: 3.87 us -> none  [the longest x1 1.3 us: shards(): bias.reshape(1, HID)]
    pallas_call x0 -> x1, Pallas kernels: none -> 3 us  [shards(): pl.pallas_call(update_kernel, out_shape=(jax.ShapeDtypeStruct((2 * OWN, H...]
where the time goes in v2:
time: 167 us
  Pallas kernels  166 us (99%)
    pallas_call x1, Pallas kernels, shards(): pl.pallas_call(kernel, out_shape=(jax.ShapeDtypeStruct((2 * OWN, HID), bf...  163 us

profile of v2, /device:TPU:8, one launch (start us, length us, event | category | flops | bytes accessed | tf_op | source)
XLA Modules:
  0.0 166.8 jit_solution(520112510652869682)
XLA Ops:
  0.6 163.2 %fused_step.1 = (bf16[128,3072]{1,0:T(8,128)(2,1)}, bf16[64,1536]{1,0:T(8,128)(2,1)}, f32[32,192]{1,0:T(8,128)}, f32[32,384]{1,0:T(8,128)}) custom-call(bf16[64,1536]{1,0:T(8,128)(2,1)} %tok.1, bf16[1536,3072]{1,0:T(8,128)(2,1)} %w_hbm.1, bf16[3072]{0:T(1024)(128)(2,1)} %bias.1, bf16[1536]{0:T(1024)(128)(2,1)} %gain.1, bf16[1536]{0:T(1024)(128)(2,1)} %shift.1, ...), custom_call_target="tpu_custom_call" | custom-call | flops 9663676416 | bytes 14000000 | tf_op jit(solution)/shard_map/fused_step/pallas_call | solution.py:788
  163.8 3.0 %adapter_update.1 = (bf16[128,3072]{1,0:T(8,128)(2,1)}, bf16[64,1536]{1,0:T(8,128)(2,1)}, f32[32,192]{1,0:T(8,128)}, f32[32,192]{1,0:T(8,128)}, f32[32,192]{1,0:...) custom-call(bf16[128,3072]{1,0:T(8,128)(2,1)} %get-tuple-element.12.hidden, ...), custom_call_target="tpu_custom_call" | custom-call | tf_op jit(solution)/shard_map/adapter_update/pallas_call | solution.py:807

commit v3 on v2

--- a/solution.py
+++ b/solution.py
@@ -32,6 +32,8 @@
 CODE_SPAN = 120.0
 LN2 = 0.6931471805599453
 TILE = 512
+WIDE = 1024
+LAST = CHUNKS - 1
 
 
 def gelu_both(v):
@@ -114,6 +116,13 @@
     ng,
     gst_s,
     gst_r,
+    xs_s,
+    xs_r,
+    sst_s,
+    sst_r,
+    sct_s,
+    sct_r,
+    stt,
     low_own,
     dn_acc,
     ugs,
@@ -134,6 +143,9 @@
     cs_sem,
     lo_sem,
     gst_sem,
+    xs_sem,
+    sst_sem,
+    sct_sem,
     ug_sem,
     dg_sem,
     ux_sem,
@@ -359,7 +371,7 @@
             return jnp.dot(low[k], u_prod[:, cols], preferred_element_type=f32)
 
         def columns(t):
-            return pl.ds(pl.multiple_of(t * TILE, TILE), TILE)
+            return pl.ds(pl.multiple_of(t * WIDE, WIDE), WIDE)
 
         def main_tile(cols):
             return jnp.dot(nrm[k], w[:, cols], preferred_element_type=f32)
@@ -374,10 +386,10 @@
                 part[k, :, columns(t)] += rank_tile(columns(t))
                 return carry
 
-            lax.fori_loop(0, HID // TILE, tile, 0)
+            lax.fori_loop(0, HID // WIDE, tile, 0)
             adapter_operands()
             rank_product()
-            lax.fori_loop(0, HID // TILE, add, 0)
+            lax.fori_loop(0, HID // WIDE, add, 0)
 
         @pl.when(k > 0)
         def _():
@@ -386,7 +398,7 @@
                 return carry
 
             rank_product()
-            lax.fori_loop(0, HID // TILE, tile, 0)
+            lax.fori_loop(0, HID // WIDE, tile, 0)
 
         rs_send(k, 0, opp, 0)
         rs_send(k, 3, opp, 1)
@@ -506,7 +518,7 @@
         def _():
             down_send()
 
-        bsize = 256
+        bsize = 768
 
         def tile(t, carry):
             rows = pl.ds(pl.multiple_of(t * bsize, bsize), bsize)
@@ -516,6 +528,10 @@
             return carry
 
         lax.fori_loop(0, FEAT // bsize, tile, 0)
+        pl.when(k < LAST)(lambda: fold_send(k))
+        pl.when(k == LAST)(last_send)
+
+    def fold_send(k):
         for j in range(1, YS):
             rows = pl.ds(pl.multiple_of(RING * ((y + j) % YS), RING), RING)
 
@@ -524,6 +540,69 @@
 
             encode(lambda t: back[k, rows, t : t + TILE], store, RING, FEAT)
             cs_copy(k, j).start()
+
+    def xs_copy(j):
+        return remote(xs_s.at[j - 1], xs_r.at[j - 1], xs_sem, (j,), {"col": (c + j) % COLS})
+
+    def sst_copy(j):
+        return remote(sst_s, sst_r.at[j - 1], sst_sem, (j,), {"row": (r + j) % ROWS})
+
+    def sct_copy(j):
+        return remote(sct_s, sct_r.at[j - 1], sct_sem, (j,), {"col": (c + j) % COLS})
+
+    def last_send():
+        for j in range(1, COLS):
+            rows = pl.ds(pl.multiple_of(STEP * ((c + j) % COLS), STEP), STEP)
+
+            def store(t, n, value):
+                xs_s[j - 1, :, t : t + n] = value
+
+            encode(lambda t: back[LAST, rows, t : t + TILE], store, STEP, FEAT)
+            xs_copy(j).start()
+        mean_, inv_ = mst[LAST, :, 0:1], mst[LAST, :, 1:2]
+        one = jnp.zeros((TOK, 1), f32)
+        two = jnp.zeros((TOK, 1), f32)
+        for t in range(0, FEAT, 256):
+            cols = slice(t, t + 256)
+            scaled = back[LAST, :, cols] * gain_row[:, cols]
+            centred = (raw[LAST, :, cols].astype(f32) - mean_) * inv_
+            one += jnp.sum(scaled, axis=1, keepdims=True)
+            two += jnp.sum(scaled * centred, axis=1, keepdims=True)
+        lanes = lax.broadcasted_iota(jnp.int32, (TOK, 128), 1)
+        sst_s[...] = jnp.where(lanes == 0, one, jnp.where(lanes == 1, two, 0.0)).T[0:8]
+        for j in range(1, ROWS):
+            sst_copy(j).start()
+
+    def last_stats():
+        for j in range(1, ROWS):
+            sst_copy(j).wait_recv()
+        sct_s[...] = sst_s[...] + sst_r[0] + sst_r[1] + sst_r[2]
+        for j in range(1, COLS):
+            sct_copy(j).start()
+
+    def last_finish():
+        for j in range(1, COLS):
+            sct_copy(j).wait_recv()
+        sums_ = sct_s[...]
+        for j in range(1, COLS):
+            sums_ += sct_r[j - 1]
+        stt[...] = (jnp.concatenate([sums_, jnp.zeros((120, 128), f32)], axis=0) * count).T
+        mine = pl.ds(pl.multiple_of(STEP * c, STEP), STEP)
+        one, two = stt[mine, 0:1], stt[mine, 1:2]
+        inv_ = mst[LAST, mine, 1:2]
+        for j in range(1, COLS):
+            xs_copy(j).wait_recv()
+        got = [
+            decoder(lambda t, n, j=j: xs_r[j - 1, :, t : t + n], FEAT) for j in range(1, COLS)
+        ]
+        for t in range(0, FEAT, TILE):
+            cols = slice(t, t + TILE)
+            value = back[LAST, mine, cols]
+            for part_ in got:
+                value += part_(t)
+            input_grad[STEP * LAST : STEP * CHUNKS, cols] = (
+                inv_ * (value * gain_row[:, cols] - one - own_centred(LAST, cols) * two)
+            ).astype(bf16)
 
     def lo_copy(k):
         return remote(lo_s.at[k], lo_r.at[k], lo_sem, (k,), {"col": pc})
@@ -642,13 +721,15 @@
         step(it == CHUNKS, up_send)
         step(it == CHUNKS + 2, drain_early)
         step((it >= 3) & (it < CHUNKS + 3), lambda: phase_backward(it - 3))
+        step((it >= CHUNKS) & (it < CHUNKS + LAST), lambda: phase_fold(it - CHUNKS))
+        step(it >= CHUNKS + 2, lambda: phase_finish(it - CHUNKS - 2))
+        step((it > CHUNKS) & (it <= CHUNKS + LAST), lambda: phase_stats(it - CHUNKS - 1))
+        step(it == CHUNKS + 2, last_stats)
         step(it == CHUNKS + 2, grads_spread)
-        step(it >= CHUNKS + 2, lambda: phase_finish(it - CHUNKS - 2))
-        step((it >= CHUNKS + 1) & (it < CHUNKS * 2 + 1), lambda: phase_stats(it - CHUNKS - 1))
-        step((it >= CHUNKS) & (it < CHUNKS * 2), lambda: phase_fold(it - CHUNKS))
+        step(it == CHUNKS + 3, last_finish)
         return carry
 
-    lax.fori_loop(0, CHUNKS * 2 + 2, iteration, 0)
+    lax.fori_loop(0, CHUNKS + LAST + 2, iteration, 0)
 
     for j in range(1, ROWS):
         ux_copy(j, (r + ROWS - j) % ROWS).wait_recv()
@@ -674,14 +755,24 @@
     def drain(k, carry):
         for j in range(1, YS):
             cs_copy(k, j).wait_send()
-        for slot, owner in ((0, r), (1, r), (2, left), (3, r), (4, r), (5, right)):
-            ag_copy(k, slot, owner).wait_send()
         lo_copy(k).wait_send()
         for j in range(1, ROWS):
             gst_copy(k, j).wait_send()
         return carry
 
-    lax.fori_loop(0, CHUNKS, drain, 0)
+    lax.fori_loop(0, LAST, drain, 0)
+
+    def drain_slopes(k, carry):
+        for slot, owner in ((0, r), (1, r), (2, left), (3, r), (4, r), (5, right)):
+            ag_copy(k, slot, owner).wait_send()
+        return carry
+
+    lax.fori_loop(0, CHUNKS, drain_slopes, 0)
+    for j in range(1, ROWS):
+        sst_copy(j).wait_send()
+    for j in range(1, COLS):
+        xs_copy(j).wait_send()
+        sct_copy(j).wait_send()
 
 
 def update_kernel(
@@ -753,13 +844,20 @@
         pltpu.VMEM((n, 6, STEP, HID + 128), bf16),
         pltpu.VMEM((n, TOK, HID), bf16),
         pltpu.VMEM((n, TOK, FEAT), f32),
-        pltpu.VMEM((n, YS - 1, RING, FEAT + 128), bf16),
-        pltpu.VMEM((n, YS - 1, RING, FEAT + 128), bf16),
-        pltpu.VMEM((n, STEP, FEAT + 128), bf16),
-        pltpu.VMEM((n, STEP, FEAT + 128), bf16),
-        pltpu.VMEM((n, STEP, FEAT), f32),
-        pltpu.VMEM((n, STEP, 128), f32),
-        pltpu.VMEM((n, ROWS - 1, STEP, 128), f32),
+        pltpu.VMEM((LAST, YS - 1, RING, FEAT + 128), bf16),
+        pltpu.VMEM((LAST, YS - 1, RING, FEAT + 128), bf16),
+        pltpu.VMEM((LAST, STEP, FEAT + 128), bf16),
+        pltpu.VMEM((LAST, STEP, FEAT + 128), bf16),
+        pltpu.VMEM((LAST, STEP, FEAT), f32),
+        pltpu.VMEM((LAST, STEP, 128), f32),
+        pltpu.VMEM((LAST, ROWS - 1, STEP, 128), f32),
+        pltpu.VMEM((COLS - 1, STEP, FEAT + 128), bf16),
+        pltpu.VMEM((COLS - 1, STEP, FEAT + 128), bf16),
+        pltpu.VMEM((8, 128), f32),
+        pltpu.VMEM((ROWS - 1, 8, 128), f32),
+        pltpu.VMEM((8, 128), f32),
+        pltpu.VMEM((COLS - 1, 8, 128), f32),
+        pltpu.VMEM((TOK, 128), f32),
         pltpu.VMEM((n, RING, 128), f32),
         pltpu.VMEM((RANK, FEAT), f32),
         pltpu.VMEM((DEPTH, RANK, UPB), f32),
@@ -777,9 +875,12 @@
         dma((2, DEPTH)),
         dma((2, n, 6)),
         dma((2, n, 6)),
-        dma((2, n, YS)),
-        dma((2, n)),
-        dma((2, n, ROWS)),
+        dma((2, LAST, YS)),
+        dma((2, LAST)),
+        dma((2, LAST, ROWS)),
+        dma((2, COLS)),
+        dma((2, ROWS)),
+        dma((2, COLS)),
         dma((2, DEPTH)),
         dma((2, DEPTH)),
         dma((2, ROWS)),

time: 167 us -> 162 us (0.970); the launches traced: 167 us -> 160 us
  Pallas kernels: 166 us -> 159 us
    pallas_call x1, Pallas kernels: 163 us -> 156 us  [shards(): pl.pallas_call(kernel, out_shape=(jax.ShapeDtypeStruct((2 * OWN, HID), bf...]
where the time goes in v3:
time: 162 us; the launch traced here: 160 us
  Pallas kernels  159 us (98%)
    pallas_call x1, Pallas kernels, shards(): pl.pallas_call(kernel, out_shape=(jax.ShapeDtypeStruct((2 * OWN, HID), bf...  156 us

profile of v3, /device:TPU:8, one launch (start us, length us, event | category | flops | bytes accessed | tf_op | source)
XLA Modules:
  0.0 159.9 jit_solution(10450391551385373452)
XLA Ops:
  0.6 156.2 %fused_step.1 = (bf16[128,3072]{1,0:T(8,128)(2,1)}, bf16[64,1536]{1,0:T(8,128)(2,1)}, f32[32,192]{1,0:T(8,128)}, f32[32,384]{1,0:T(8,128)}) custom-call(bf16[64,1536]{1,0:T(8,128)(2,1)} %tok.1, bf16[1536,3072]{1,0:T(8,128)(2,1)} %w_hbm.1, bf16[3072]{0:T(1024)(128)(2,1)} %bias.1, bf16[1536]{0:T(1024)(128)(2,1)} %gain.1, bf16[1536]{0:T(1024)(128)(2,1)} %shift.1, ...), custom_call_target="tpu_custom_call" | custom-call | flops 9663676416 | bytes 14000000 | tf_op jit(solution)/shard_map/fused_step/pallas_call | solution.py:889
  156.9 3.0 %adapter_update.1 = (bf16[128,3072]{1,0:T(8,128)(2,1)}, bf16[64,1536]{1,0:T(8,128)(2,1)}, f32[32,192]{1,0:T(8,128)}, f32[32,192]{1,0:T(8,128)}, f32[32,192]{1,0:...) custom-call(bf16[128,3072]{1,0:T(8,128)(2,1)} %get-tuple-element.12.hidden, ...), custom_call_target="tpu_custom_call" | custom-call | tf_op jit(solution)/shard_map/adapter_update/pallas_call | solution.py:908

commit v4 on v3

--- a/solution.py
+++ b/solution.py
@@ -33,6 +33,7 @@
 LN2 = 0.6931471805599453
 TILE = 512
 WIDE = 1024
+HALF = FEAT // 2
 LAST = CHUNKS - 1
 
 
@@ -57,20 +58,20 @@
     return weight - learn_rate * (update + decay_rate * weight), new_moment, new_square
 
 
-def encode(load, store, rows, width):
+def encode(load, store, rows, width, tile=TILE):
     top = jnp.zeros((rows, 1), f32)
-    for t in range(0, width, TILE):
+    for t in range(0, width, tile):
         top = jnp.maximum(top, jnp.max(jnp.abs(load(t)), axis=1, keepdims=True))
     top = (jnp.maximum(top, 1e-30) * 1.01).astype(bf16)
     factor = CODE_SPAN / top.astype(f32)
-    for t in range(0, width, TILE):
-        store(t, TILE, jnp.exp2(load(t) * factor).astype(bf16))
+    for t in range(0, width, tile):
+        store(t, tile, jnp.exp2(load(t) * factor).astype(bf16))
     store(width, 128, jnp.broadcast_to(top, (rows, 128)))
 
 
-def decoder(load, width):
+def decoder(load, width, tile=TILE):
     scale = load(width, 128)[:, 0:1].astype(f32) * (1.0 / (CODE_SPAN * LN2))
-    return lambda t: jnp.log(load(t, TILE).astype(f32)) * scale
+    return lambda t: jnp.log(load(t, tile).astype(f32)) * scale
 
 
 def kernel(
@@ -89,6 +90,7 @@
     w,
     cot,
     local_sem,
+    hid,
     stat_s,
     stat_r,
     gain_row,
@@ -170,6 +172,7 @@
 
     w_copy = pltpu.make_async_copy(w_hbm, w, local_sem.at[0])
     cot_copy = pltpu.make_async_copy(cot_hbm, cot, local_sem.at[1])
+    hid_copy = pltpu.make_async_copy(hid, hidden, local_sem.at[2])
     w_copy.start()
     cot_copy.start()
 
@@ -439,7 +442,7 @@
                 cols = slice(t, t + TILE)
                 v = part[kk, rows, cols] + one(t) + two(t) + bias_row[:, cols]
                 value, slope = gelu_both(v)
-                hidden[pl.ds(start, STEP), cols] = value.astype(bf16)
+                hid[pl.ds(start, STEP), cols] = value.astype(bf16)
                 slg[kk, rows, cols] = (
                     cot[pl.ds(start, STEP), cols].astype(f32) * slope
                 ).astype(bf16)
@@ -476,6 +479,7 @@
             dg_copy(j).start()
 
     def up_send():
+        hid_copy.start()
         lanes = lax.broadcasted_iota(jnp.int32, (RING, 128), 1)
         sides = []
         for k in range(CHUNKS):
@@ -518,7 +522,7 @@
         def _():
             down_send()
 
-        bsize = 768
+        bsize = HALF
 
         def tile(t, carry):
             rows = pl.ds(pl.multiple_of(t * bsize, bsize), bsize)
@@ -527,9 +531,20 @@
             ) + jnp.dot(rank, d_prod[:, rows], preferred_element_type=f32)
             return carry
 
-        lax.fori_loop(0, FEAT // bsize, tile, 0)
-        pl.when(k < LAST)(lambda: fold_send(k))
-        pl.when(k == LAST)(last_send)
+        @pl.when(k < LAST)
+        def _():
+            lax.fori_loop(0, FEAT // bsize, tile, 0)
+            fold_send(k)
+
+        @pl.when(k == LAST)
+        def _():
+            def both_steps(half, carry):
+                tile(half, carry)
+                last_send(half)
+                return carry
+
+            lax.fori_loop(0, FEAT // bsize, both_steps, 0)
+            last_sums()
 
     def fold_send(k):
         for j in range(1, YS):
@@ -541,8 +556,14 @@
             encode(lambda t: back[k, rows, t : t + TILE], store, RING, FEAT)
             cs_copy(k, j).start()
 
-    def xs_copy(j):
-        return remote(xs_s.at[j - 1], xs_r.at[j - 1], xs_sem, (j,), {"col": (c + j) % COLS})
+    def xs_copy(half, j):
+        return remote(
+            xs_s.at[half, j - 1],
+            xs_r.at[half, j - 1],
+            xs_sem,
+            (half, j),
+            {"col": (c + j) % COLS},
+        )
 
     def sst_copy(j):
         return remote(sst_s, sst_r.at[j - 1], sst_sem, (j,), {"row": (r + j) % ROWS})
@@ -550,15 +571,20 @@
     def sct_copy(j):
         return remote(sct_s, sct_r.at[j - 1], sct_sem, (j,), {"col": (c + j) % COLS})
 
-    def last_send():
+    def last_send(half):
         for j in range(1, COLS):
             rows = pl.ds(pl.multiple_of(STEP * ((c + j) % COLS), STEP), STEP)
 
+            def load(t):
+                return back[LAST, rows, pl.ds(pl.multiple_of(HALF * half + t, 256), 256)]
+
             def store(t, n, value):
-                xs_s[j - 1, :, t : t + n] = value
-
-            encode(lambda t: back[LAST, rows, t : t + TILE], store, STEP, FEAT)
-            xs_copy(j).start()
+                xs_s[half, j - 1, :, t : t + n] = value
+
+            encode(load, store, STEP, HALF, 256)
+            xs_copy(half, j).start()
+
+    def last_sums():
         mean_, inv_ = mst[LAST, :, 0:1], mst[LAST, :, 1:2]
         one = jnp.zeros((TOK, 1), f32)
         two = jnp.zeros((TOK, 1), f32)
@@ -590,19 +616,21 @@
         mine = pl.ds(pl.multiple_of(STEP * c, STEP), STEP)
         one, two = stt[mine, 0:1], stt[mine, 1:2]
         inv_ = mst[LAST, mine, 1:2]
-        for j in range(1, COLS):
-            xs_copy(j).wait_recv()
-        got = [
-            decoder(lambda t, n, j=j: xs_r[j - 1, :, t : t + n], FEAT) for j in range(1, COLS)
-        ]
-        for t in range(0, FEAT, TILE):
-            cols = slice(t, t + TILE)
-            value = back[LAST, mine, cols]
-            for part_ in got:
-                value += part_(t)
-            input_grad[STEP * LAST : STEP * CHUNKS, cols] = (
-                inv_ * (value * gain_row[:, cols] - one - own_centred(LAST, cols) * two)
-            ).astype(bf16)
+        for half in range(2):
+            for j in range(1, COLS):
+                xs_copy(half, j).wait_recv()
+            got = [
+                decoder(lambda t, n, j=j: xs_r[half, j - 1, :, t : t + n], HALF, 256)
+                for j in range(1, COLS)
+            ]
+            for t in range(0, HALF, 256):
+                cols = slice(HALF * half + t, HALF * half + t + 256)
+                value = back[LAST, mine, cols]
+                for part_ in got:
+                    value += part_(t)
+                input_grad[STEP * LAST : STEP * CHUNKS, cols] = (
+                    inv_ * (value * gain_row[:, cols] - one - own_centred(LAST, cols) * two)
+                ).astype(bf16)
 
     def lo_copy(k):
         return remote(lo_s.at[k], lo_r.at[k], lo_sem, (k,), {"col": pc})
@@ -744,6 +772,7 @@
     up_grad[...] = up_gradient
     down_grad[...] = down_gradient
 
+    hid_copy.wait()
     for j in range(1, ROWS):
         ux_copy(j, r).wait_send()
     for j in range(1, COLS):
@@ -771,7 +800,8 @@
     for j in range(1, ROWS):
         sst_copy(j).wait_send()
     for j in range(1, COLS):
-        xs_copy(j).wait_send()
+        xs_copy(0, j).wait_send()
+        xs_copy(1, j).wait_send()
         sct_copy(j).wait_send()
 
 
@@ -823,7 +853,8 @@
     scratch = [
         pltpu.VMEM((FEAT, HID), bf16),
         pltpu.VMEM((2 * OWN, HID), bf16),
-        dma((2,)),
+        dma((3,)),
+        pltpu.VMEM((2 * OWN, HID), bf16),
         pltpu.VMEM((8, 128), f32),
         pltpu.VMEM((ROWS - 1, 8, 128), f32),
         pltpu.VMEM((1, FEAT), f32),
@@ -851,8 +882,8 @@
         pltpu.VMEM((LAST, STEP, FEAT), f32),
         pltpu.VMEM((LAST, STEP, 128), f32),
         pltpu.VMEM((LAST, ROWS - 1, STEP, 128), f32),
-        pltpu.VMEM((COLS - 1, STEP, FEAT + 128), bf16),
-        pltpu.VMEM((COLS - 1, STEP, FEAT + 128), bf16),
+        pltpu.VMEM((2, COLS - 1, STEP, HALF + 128), bf16),
+        pltpu.VMEM((2, COLS - 1, STEP, HALF + 128), bf16),
         pltpu.VMEM((8, 128), f32),
         pltpu.VMEM((ROWS - 1, 8, 128), f32),
         pltpu.VMEM((8, 128), f32),
@@ -878,7 +909,7 @@
         dma((2, LAST, YS)),
         dma((2, LAST)),
         dma((2, LAST, ROWS)),
-        dma((2, COLS)),
+        dma((2, 2, COLS)),
         dma((2, ROWS)),
         dma((2, COLS)),
         dma((2, DEPTH)),
@@ -895,7 +926,7 @@
             wide,
         ),
         in_specs=[vmem, hbm] + [vmem] * 5 + [hbm],
-        out_specs=(vmem,) * 4,
+        out_specs=(hbm,) + (vmem,) * 3,
         scratch_shapes=scratch,
         compiler_params=pltpu.CompilerParams(
             collective_id=0, has_side_effects=True, vmem_limit_bytes=56 * 1024 * 1024

time: 162 us -> 163 us (level)
  no operation moved by 1% of the time
where the time goes in v4:
time: 163 us; the launch traced here: 160 us
  Pallas kernels  159 us (98%)
    pallas_call x1, Pallas kernels, shards(): pl.pallas_call(kernel, out_shape=(jax.ShapeDtypeStruct((2 * OWN, HID), bf...  156 us

profile of v4, /device:TPU:8, one launch (start us, length us, event | category | flops | bytes accessed | tf_op | source)
XLA Modules:
  0.0 159.8 jit_solution(1147441010049368315)
XLA Ops:
  0.6 156.1 %fused_step.1 = (bf16[128,3072]{1,0:T(8,128)(2,1)}, bf16[64,1536]{1,0:T(8,128)(2,1)}, f32[32,192]{1,0:T(8,128)}, f32[32,384]{1,0:T(8,128)}) custom-call(bf16[64,1536]{1,0:T(8,128)(2,1)} %tok.1, bf16[1536,3072]{1,0:T(8,128)(2,1)} %w_hbm.1, bf16[3072]{0:T(1024)(128)(2,1)} %bias.1, bf16[1536]{0:T(1024)(128)(2,1)} %gain.1, bf16[1536]{0:T(1024)(128)(2,1)} %shift.1, ...), custom_call_target="tpu_custom_call" | custom-call | flops 9663676416 | bytes 14000000 | tf_op jit(solution)/shard_map/fused_step/pallas_call | solution.py:920
  156.8 3.0 %adapter_update.1 = (bf16[128,3072]{1,0:T(8,128)(2,1)}, bf16[64,1536]{1,0:T(8,128)(2,1)}, f32[32,192]{1,0:T(8,128)}, f32[32,192]{1,0:T(8,128)}, f32[32,192]{1,0:...) custom-call(bf16[128,3072]{1,0:T(8,128)(2,1)} %get-tuple-element.12.hidden, ...), custom_call_target="tpu_custom_call" | custom-call | tf_op jit(solution)/shard_map/adapter_update/pallas_call | solution.py:939

commit v5 on v3

--- a/solution.py
+++ b/solution.py
@@ -89,6 +89,7 @@
     w,
     cot,
     local_sem,
+    hid,
     stat_s,
     stat_r,
     gain_row,
@@ -170,6 +171,7 @@
 
     w_copy = pltpu.make_async_copy(w_hbm, w, local_sem.at[0])
     cot_copy = pltpu.make_async_copy(cot_hbm, cot, local_sem.at[1])
+    hid_copy = pltpu.make_async_copy(hid, hidden, local_sem.at[2])
     w_copy.start()
     cot_copy.start()
 
@@ -439,7 +441,7 @@
                 cols = slice(t, t + TILE)
                 v = part[kk, rows, cols] + one(t) + two(t) + bias_row[:, cols]
                 value, slope = gelu_both(v)
-                hidden[pl.ds(start, STEP), cols] = value.astype(bf16)
+                hid[pl.ds(start, STEP), cols] = value.astype(bf16)
                 slg[kk, rows, cols] = (
                     cot[pl.ds(start, STEP), cols].astype(f32) * slope
                 ).astype(bf16)
@@ -476,6 +478,7 @@
             dg_copy(j).start()
 
     def up_send():
+        hid_copy.start()
         lanes = lax.broadcasted_iota(jnp.int32, (RING, 128), 1)
         sides = []
         for k in range(CHUNKS):
@@ -500,6 +503,12 @@
         ag_copy(k, 4, right).wait_recv()
         ag_copy(k, 2, opp).wait_recv()
         ag_copy(k, 5, opp).wait_recv()
+
+        @pl.when(k == LAST)
+        def _():
+            for j in range(1, ROWS):
+                ux_copy(j, r).start()
+
         slopes = slg[k]
         rank = split(
             adapter_scale * lax.dot_general(slopes, u_low[...], NT, preferred_element_type=f32)
@@ -660,18 +669,19 @@
                 inv_ * (ng[k, :, cols] - sums[:, 0:1] - own_centred(k, cols) * sums[:, 1:2])
             ).astype(bf16)
 
+    def up_sum():
+        total_ = ugs[d]
+        for j in range(1, DEPTH):
+            ug_copy(j).wait_recv()
+            total_ += ugr[j]
+        upx[r] = total_
+
     def grads_spread():
-        up_sum = ugs[d]
         dn_sum = dgs[d]
         for j in range(1, DEPTH):
-            ug_copy(j).wait_recv()
             dg_copy(j).wait_recv()
-            up_sum += ugr[j]
             dn_sum += dgr[j]
-        upx[r] = up_sum
         dnx[c] = dn_sum
-        for j in range(1, ROWS):
-            ux_copy(j, r).start()
         for j in range(1, COLS):
             dx_copy(j, c).start()
 
@@ -721,6 +731,7 @@
         step(it == CHUNKS, up_send)
         step(it == CHUNKS + 2, drain_early)
         step((it >= 3) & (it < CHUNKS + 3), lambda: phase_backward(it - 3))
+        step(it == CHUNKS + 1, up_sum)
         step((it >= CHUNKS) & (it < CHUNKS + LAST), lambda: phase_fold(it - CHUNKS))
         step(it >= CHUNKS + 2, lambda: phase_finish(it - CHUNKS - 2))
         step((it > CHUNKS) & (it <= CHUNKS + LAST), lambda: phase_stats(it - CHUNKS - 1))
@@ -744,6 +755,7 @@
     up_grad[...] = up_gradient
     down_grad[...] = down_gradient
 
+    hid_copy.wait()
     for j in range(1, ROWS):
         ux_copy(j, r).wait_send()
     for j in range(1, COLS):
@@ -823,7 +835,8 @@
     scratch = [
         pltpu.VMEM((FEAT, HID), bf16),
         pltpu.VMEM((2 * OWN, HID), bf16),
-        dma((2,)),
+        dma((3,)),
+        pltpu.VMEM((2 * OWN, HID), bf16),
         pltpu.VMEM((8, 128), f32),
         pltpu.VMEM((ROWS - 1, 8, 128), f32),
         pltpu.VMEM((1, FEAT), f32),
@@ -895,7 +908,7 @@
             wide,
         ),
         in_specs=[vmem, hbm] + [vmem] * 5 + [hbm],
-        out_specs=(vmem,) * 4,
+        out_specs=(hbm,) + (vmem,) * 3,
         scratch_shapes=scratch,
         compiler_params=pltpu.CompilerParams(
             collective_id=0, has_side_effects=True, vmem_limit_bytes=56 * 1024 * 1024

time: 162 us -> 159 us (0.981)
  no operation moved by 1% of the time
where the time goes in v5:
time: 159 us; the launch traced here: 158 us
  Pallas kernels  158 us (99%)
    pallas_call x1, Pallas kernels, shards(): pl.pallas_call(kernel, out_shape=(jax.ShapeDtypeStruct((2 * OWN, HID), bf...  155 us

profile of v5, /device:TPU:8, one launch (start us, length us, event | category | flops | bytes accessed | tf_op | source)
XLA Modules:
  0.0 158.5 jit_solution(3748853030552438349)
XLA Ops:
  0.6 154.8 %fused_step.1 = (bf16[128,3072]{1,0:T(8,128)(2,1)}, bf16[64,1536]{1,0:T(8,128)(2,1)}, f32[32,192]{1,0:T(8,128)}, f32[32,384]{1,0:T(8,128)}) custom-call(bf16[64,1536]{1,0:T(8,128)(2,1)} %tok.1, bf16[1536,3072]{1,0:T(8,128)(2,1)} %w_hbm.1, bf16[3072]{0:T(1024)(128)(2,1)} %bias.1, bf16[1536]{0:T(1024)(128)(2,1)} %gain.1, bf16[1536]{0:T(1024)(128)(2,1)} %shift.1, ...), custom_call_target="tpu_custom_call" | custom-call | flops 9663676416 | bytes 14000000 | tf_op jit(solution)/shard_map/fused_step/pallas_call | solution.py:902
  155.4 3.0 %adapter_update.1 = (bf16[128,3072]{1,0:T(8,128)(2,1)}, bf16[64,1536]{1,0:T(8,128)(2,1)}, f32[32,192]{1,0:T(8,128)}, f32[32,192]{1,0:T(8,128)}, f32[32,192]{1,0:...) custom-call(bf16[128,3072]{1,0:T(8,128)(2,1)} %get-tuple-element.12.hidden, ...), custom_call_target="tpu_custom_call" | custom-call | tf_op jit(solution)/shard_map/adapter_update/pallas_call | solution.py:921
